TPU v7x, 32 devices: a whole 2x2x4 slice. The times are simulated.
32 devices in a mesh: dp: 4 (over y, core), slab: 8 (over z, x).
Axes of the slice: x: 2, y: 2, z: 4, core: 2. Of those that a mesh axis runs over, the one named last changes fastest.
Arguments:
- features: bfloat16 [4, 80, 64, 256], P('dp', 'slab'), may hold values from -6 to 6
- cotangent: bfloat16 [4, 80, 64, 256], P('dp', 'slab'), may hold values from -6 to 6
- neighbour_table: int32 [4, 80, 27], P('dp', 'slab'), may hold values from 0 to 14, as said below
- send_lists: int32 [4, 8, 2, 2], P('dp', 'slab'), may hold values from 0 to 10, as said below
- block_counts: int32 [4, 8], P('dp', 'slab'), may hold values from 5 to 10, as said below
- weight_one: bfloat16 [6912, 256], replicated, may hold values from -0.078125 to 0.078125
- weight_two: bfloat16 [6912, 256], replicated, may hold values from -0.078125 to 0.078125
Outputs:
- output: bfloat16 [4, 80, 64, 256], P('dp', 'slab')
- grad_features: bfloat16 [4, 80, 64, 256], P('dp', 'slab')
- grad_one: float32 [6912, 256], P('slab', 'dp')
- grad_two: float32 [6912, 256], P('slab', 'dp')
Inputs may be any that keep to these rules, and one draw needn't show every extreme that they name: `neighbour_table`: row b of slab l = b // 10 lists where the block at each of the 27 block offsets lies, in the numbering of the gathered step; rows of padding slots hold only 14. The relation is symmetric: a block that names another at an offset is named by it at the opposite offset. `send_lists`: list 0 of a slab names, in increasing order, its occupied blocks in its first block-plane, the ones the previous slab can touch; list 1 those of its last block-plane; 10 fills the remaining slots. `block_counts`: slots at and above a slab's count are padding.
All inputs are finite; a program needn't handle non-finite values.
Results may differ from a plain program's by a relative error of at most 0.013.
Values may be sent and summed in bfloat16 or wider, within the bound.
No kernel may reach another device: no remote copies, remote signals or barrier semaphores. Data moves between devices by JAX's collectives and lax.ppermute only.
A program may use at most 128 MiB of HBM per device.

v0:
```python
import functools
import math

import jax
import jax.numpy as jnp
from jax import lax
from jax.experimental import pallas as pl
from jax.experimental.pallas import tpu as pltpu
from jax.sharding import PartitionSpec as P

F32 = jnp.float32
BF16 = jnp.bfloat16
TAPS = 27
ROWS = 16
MIB = 2**20
SECOND_COST = 1
INNER_LIMIT = 44
FORWARD_LIMIT = 14
UNROLL = 5

ORDERS_ONE = (
    (0, 288, ("x", "y", "z1")),
    (288, 432, ("y", "x", "z1")),
)
ORDERS_TWO = (
    (0, 256, ("z1", "y", "x")),
    (256, 432, ("y", "z1", "x")),
)
LAST = "z2"


def shift_matrix():
    shape = (8 * ROWS, 9 * ROWS)
    row = lax.broadcasted_iota(jnp.int32, shape, 0)
    column = lax.broadcasted_iota(jnp.int32, shape, 1)
    shift = row >> 4
    shift = jnp.where(shift >= 4, shift + 1, shift)
    across = jnp.where(shift >= 6, 2, jnp.where(shift >= 3, 1, 0))
    y = ((row >> 2) & 3) + across + 3
    z = (row & 3) + (shift - 3 * across) + 3
    plane = 3 * (y >> 2) + (z >> 2)
    source = 16 * plane + 4 * (y & 3) + (z & 3)
    return jnp.where(column == source, 1.0, 0.0).astype(BF16)


def bit_of(name, dp_index, slab_index):
    if name == "y":
        return dp_index // 2
    if name == "x":
        return slab_index % 2
    if name == "z1":
        return slab_index // 2 % 2
    return slab_index // 4


def pair_perm(name, dp_size, slab_size):
    dp_flip = {"core": 1, "y": 2}.get(name, 0)
    slab_flip = {"x": 1, "z1": 2, "z2": 4}.get(name, 0)
    return [
        (d * slab_size + s, (d ^ dp_flip) * slab_size + (s ^ slab_flip))
        for d in range(dp_size)
        for s in range(slab_size)
    ]


def swap(array, name):
    dp_size, slab_size = lax.axis_size("dp"), lax.axis_size("slab")
    return lax.ppermute(array, ("dp", "slab"), pair_perm(name, dp_size, slab_size))


def swap_halos(first, second):
    count = lax.axis_size("slab")
    even = [(s, s ^ 1) for s in range(count) if s ^ 1 < count]
    odd = [(s, s + 1 if s % 2 else s - 1) for s in range(1, count) if s % 2 == 0 or s + 1 < count]
    return lax.ppermute(first, "slab", even), lax.ppermute(second, "slab", odd)


def pack_kernel(lists, features, cotangent, first, second, shift, planes, more, sems):
    blocks, channels = features.shape[1], features.shape[3]
    copies = start_planes(planes, features, blocks, sems.at[0])
    copies += start_planes(more, cotangent, blocks, sems.at[1])
    shift[...] = shift_matrix()
    for field in (planes, more):
        field[:, blocks:] = jnp.zeros_like(field[:, blocks:])
    for copy in copies:
        copy.wait()
    pack_edges(lists, (planes, more), blocks, first, second)


def pack_edges(lists, fields, blocks, first, second):
    channels = fields[0].shape[3]
    odd = lax.rem(lax.axis_index("slab"), 2)
    for q in range(lists.shape[3]):
        for ref, side in ((first, 1 - odd), (second, odd)):
            block = lists[0, 0, side, q]
            inside = jnp.minimum(block, blocks - 1)
            for part, source in enumerate(fields):
                value = source[3 * side, inside]
                ref[q, :, part * channels : (part + 1) * channels] = jnp.where(
                    block < blocks, value, jnp.zeros_like(value)
                )


def start_planes(planes, source, blocks, sem):
    copies = []
    for x in range(4):
        if source.shape[2] != ROWS:
            piece = source.at[0, :, pl.ds(x * ROWS, ROWS), :]
        else:
            piece = source.at[x]
        copies.append(pltpu.make_async_copy(piece, planes.at[x, pl.ds(0, blocks)], sem.at[x]))
        copies[-1].start()
    return copies


def fill_edges(planes, blocks, got_first, got_second, lanes, places):
    edge = got_first.shape[0]
    planes[:, blocks:] = jnp.zeros_like(planes[:, blocks:])
    is_odd = lax.rem(lax.axis_index("slab"), 2) == 1
    for q in range(edge):
        one, two = got_first[q, :, lanes], got_second[q, :, lanes]
        planes[places[0], blocks + q] = jnp.where(is_odd, one, two)
        planes[places[1], blocks + edge + q] = jnp.where(is_odd, two, one)


def gather_shifts(shifted, planes, table, shift, blocks, wanted):
    matrix = shift[...]

    def one_block(b, carry):
        for place, (at, slab) in enumerate(wanted):
            near_x = 0 if at == 0 else 2 if at == 5 else 1
            around = [planes[slab, table[0, b, 9 * near_x + n]] for n in range(9)]
            moved = jnp.dot(
                matrix, jnp.concatenate(around, axis=0), preferred_element_type=F32
            ).astype(BF16)
            pieces = [moved[n * ROWS : (n + 1) * ROWS] for n in range(8)]
            pieces.insert(4, around[4])
            for n, piece in enumerate(pieces):
                start = place * blocks * ROWS + b * ROWS
                shifted[n, pl.ds(pl.multiple_of(start, ROWS), ROWS), :] = piece
        return carry

    lax.fori_loop(0, blocks, one_block, 0, unroll=UNROLL)


INNER = ((1, 0), (2, 1), (3, 2), (4, 3))
OUTER = ((0, 0), (5, 1))


def inner_taps(inner, offset):
    step = inner.shape[1] // 4
    along_x, along_yz = offset // 9, offset % 9
    if along_x == 0:
        return inner[along_yz, : 3 * step, :], step
    return inner[along_yz, (along_x - 1) * step :, :], 0


def taps_of(inner, outer, offset):
    step = inner.shape[1] // 4
    along_x, along_yz = offset // 9, offset % 9
    own, _ = inner_taps(inner, offset)
    if along_x == 0:
        return jnp.concatenate([outer[along_yz, :step, :], own], axis=0)
    if along_x == 2:
        return jnp.concatenate([own, outer[along_yz, step:, :]], axis=0)
    return own


def tap_weight(weight, offset, flipped):
    channels = weight.shape[1]
    row = (TAPS - 1 - offset if flipped else offset) * channels
    return weight[row : row + channels, :]


def times(left, right, flipped):
    return lax.dot_general(
        left, right, (((1,), (1 if flipped else 0,)), ((), ())), preferred_element_type=F32
    )


def convolve(total, inner, outer, weight, flipped):
    order = list(range(9, 18)) + list(range(9)) + list(range(18, 27))
    for at, offset in enumerate(order):
        if outer is None:
            taps, first = inner_taps(inner, offset)
        else:
            taps, first = taps_of(inner, outer, offset), 0
        term = times(taps, tap_weight(weight, offset, flipped), flipped)
        if at == 0:
            total[...] = term
        else:
            total[first : first + term.shape[0], :] += term


def emit_share(grad, dest, portions, outs, tile_rows, slab_size):
    half = tile_rows // 2
    dp_index, slab_index = lax.axis_index("dp"), lax.axis_index("slab")
    core = lax.rem(dp_index, 2)
    lane = lax.broadcasted_iota(jnp.int32, (half, 128), 1)
    low = (lane < 64) == (core == 0)
    for y in range(2):
        upper = grad[dest * tile_rows : dest * tile_rows + half, y * 128 : (y + 1) * 128]
        lower = grad[dest * tile_rows + half : (dest + 1) * tile_rows, y * 128 : (y + 1) * 128]
        lower = pltpu.roll(lower, 64, 1)
        keep = jnp.where(low, upper, lower).astype(BF16)
        send = jnp.where(low, lower, upper).astype(BF16)
        keep_ref, send_ref = outs
        for first, last, order in portions:
            index = 0
            for name in order + (LAST,):
                bit = bit_of(name, dp_index, slab_index)
                mine = y if name == "y" else bit_of(name, 0, dest)
                index = index * 2 + (bit ^ mine)
            keep_ref[index, first:last] = keep[first:last]
            send_ref[index, first:last] = send[first:last]


def emit_gradient(product, grad, portions, outs, packed):
    channels = grad.shape[1]
    if not packed:
        for offset in range(TAPS):
            outs[0][offset * channels : (offset + 1) * channels, :] = product(offset)
        return
    slab_size = packed
    tile_rows = TAPS * channels // slab_size
    done = 0
    for offset in range(TAPS):
        grad[offset * channels : (offset + 1) * channels, :] = product(offset)
        while done < slab_size and (done + 1) * tile_rows <= (offset + 1) * channels:
            emit_share(grad, done, portions, outs, tile_rows, slab_size)
            done += 1


def over_voxels(left, right):
    return lax.dot_general(left, right, (((0,), (0,)), ((), ())), preferred_element_type=F32)


def inner_kernel(table, planes, more, shift, weight, inner, other, before, held, sem):
    blocks = before.shape[0] // 64
    fetch = pltpu.make_async_copy(weight, held, sem)
    fetch.start()
    gather_shifts(inner, planes, table, shift, blocks, INNER)
    gather_shifts(other, more, table, shift, blocks, INNER)
    fetch.wait()
    convolve(before, inner, None, held, False)


def forward_kernel(
    packed,
    portions,
    table,
    source,
    source_other,
    got_first,
    got_second,
    shift,
    weight,
    inner,
    other,
    before,
    hidden,
    outer,
    outer_other,
    *rest,
):
    *outs, planes, grad, held, sem = rest
    fetch = pltpu.make_async_copy(weight, held, sem)
    fetch.start()
    blocks, channels = hidden.shape[1], hidden.shape[3]
    step = blocks * ROWS
    for part, (field, target) in enumerate(((source, outer), (source_other, outer_other))):
        planes[0] = field[3]
        planes[1] = field[0]
        fill_edges(
            planes, blocks, got_first, got_second, pl.ds(part * channels, channels), (0, 1)
        )
        gather_shifts(target, planes, table, shift, blocks, OUTER)
    fetch.wait()
    for x in range(4):
        value = before[x * step : (x + 1) * step, :]
        if x in (0, 3):
            for n in range(9):
                taps = outer[n, :step, :] if x == 0 else outer[n, step:, :]
                value += times(taps, tap_weight(held, n if x == 0 else 18 + n, False), False)
        hidden[x] = jnp.maximum(value, 0.0).astype(BF16).reshape(hidden.shape[1:])
    left = hidden[...].reshape(4 * step, channels)
    emit_gradient(
        lambda offset: over_voxels(left, taps_of(other, outer_other, TAPS - 1 - offset)),
        grad,
        portions,
        outs,
        packed,
    )


def middle_kernel(
    lists, inner, outer, weight, hidden, grad_hidden, first, second, total
):
    blocks, channels = hidden.shape[1], hidden.shape[3]
    convolve(total, inner, outer, weight, True)
    kept = jnp.where(hidden[...].reshape(total.shape).astype(F32) > 0, total[...], 0.0)
    grad_hidden[...] = kept.astype(BF16).reshape(grad_hidden.shape)
    pack_edges(lists, (hidden, grad_hidden), blocks, first, second)


def backward_kernel(packed, portions, inner, outer, grad_hidden, *rest):
    *outs, grad = rest
    blocks, channels = grad_hidden.shape[1], grad_hidden.shape[3]
    right = grad_hidden[...].reshape(blocks * 64, channels)
    emit_gradient(
        lambda offset: over_voxels(taps_of(inner, outer, offset), right),
        grad,
        portions,
        outs,
        packed,
    )


def second_kernel(
    part, flipped, tokens, table, counts, source, got_first, got_second, shift, weight, rows, *rest
):
    out, planes, own, inner, outer, total, sem = rest[tokens:]
    blocks, channels = rows.shape[1], rows.shape[3]
    later = pltpu.make_async_copy(rows.at[0], own, sem)
    later.start()
    planes[:, :blocks] = source[...]
    fill_edges(
        planes, blocks, got_first, got_second, pl.ds(part * channels, channels), (3, 0)
    )
    gather_shifts(inner, planes, table, shift, blocks, INNER)
    gather_shifts(outer, planes, table, shift, blocks, ((0, 3), (5, 0)))
    convolve(total, inner, outer, weight, flipped)
    later.wait()
    for b in range(blocks):
        present = (b < counts[0, 0]).astype(F32)
        for x in range(4):
            at = slice(x * ROWS, (x + 1) * ROWS)
            added = own[b, at, :].astype(F32)
            start = (x * blocks + b) * ROWS
            term = total[start : start + ROWS, :]
            value = (added + term) * present if flipped else added * present + term
            out[0, b, at, :] = value.astype(BF16)


def unpack_kernel(factor, *refs):
    ins, outs = refs[:-2], refs[-2:]
    core = lax.rem(lax.axis_index("dp"), 2)
    for keep, got, out in zip(ins[0::2], ins[1::2], outs):
        columns = out.shape[0]
        whole = (keep[...].astype(F32) + got[...].astype(F32)) * factor
        whole = jnp.where(core == 0, whole, pltpu.roll(whole, columns, 1)).T
        out[...] = jnp.concatenate([whole[:columns], whole[columns:]], axis=1)


def call(kernel, outs, ins, places, scratch=(), limit=24, flops=0):
    spaces = {"s": pltpu.SMEM, "v": pltpu.VMEM, "a": pl.ANY, "h": pltpu.HBM}
    return pl.pallas_call(
        kernel,
        out_shape=outs,
        in_specs=[pl.BlockSpec(memory_space=spaces[place]) for place in places],
        out_specs=[pl.BlockSpec(memory_space=pltpu.VMEM) for _ in outs],
        scratch_shapes=list(scratch),
        compiler_params=pltpu.CompilerParams(vmem_limit_bytes=limit * MIB),
        cost_estimate=pl.CostEstimate(flops=flops, bytes_accessed=0, transcendentals=0),
    )(*ins)


def halves(array):
    half = array.shape[0] // 2
    return array[:half], array[half:]


def add_terms(parts):
    pairs = [halves(keep + got) for keep, got in parts]
    return [keep for keep, _ in pairs], [send for _, send in pairs]


def swaps(keeps, sends, names):
    return [[keep, swap(send, name)] for keep, send, name in zip(keeps, sends, names)]


def join(parts):
    return [[jnp.concatenate([part[i] for part in parts], axis=1) for i in range(2)]]


def fence(parts, others):
    keeps, others = lax.optimization_barrier(([keep for keep, _ in parts], others))
    return [[keep, got] for keep, (_, got) in zip(keeps, parts)], others


def reduce_packed(shares_one, shares_two, edges, finish):
    two, one = (
        [[keep[:, first:last], got[:, first:last]] for first, last, _ in orders]
        for keep, got, orders in (
            (shares_two[0], swap(shares_two[1], "core"), ORDERS_TWO),
            (shares_one[0], swap(shares_one[1], "core"), ORDERS_ONE),
        )
    )
    names_two = list(zip(*(order for _, _, order in ORDERS_TWO)))
    names_one = list(zip(*(order for _, _, order in ORDERS_ONE)))
    results = []
    halos = swap_halos(*edges)
    for step in range(2):
        keeps, sends = add_terms(two)
        one, sends = fence(one, sends)
        two = swaps(keeps, sends, names_two[step])
        keeps, sends = add_terms(one)
        one = swaps(keeps, sends, names_one[step])
        results.append(finish(step, sends, halos))
        two, results[-1] = fence(two, results[-1])
    keeps, sends = add_terms(join(two))
    one, sends = fence(one, sends)
    two = swaps(keeps, sends, names_two[2][:1])
    keeps, sends = add_terms(join(one))
    two, sends = fence(two, sends)
    one = swaps(keeps, sends, names_one[2][:1])
    keeps, sends = add_terms(two)
    one, sends = fence(one, sends)
    two = swaps(keeps, sends, [LAST])
    keeps, sends = add_terms(one)
    one = swaps(keeps, sends, [LAST])
    return [term[0] for term in one[0] + two[0]], results


def per_device(
    features, cotangent, neighbour_table, send_lists, block_counts, weight_one, weight_two
):
    blocks, channels = features.shape[1], features.shape[3]
    dp_size, slab_size = lax.axis_size("dp"), lax.axis_size("slab")
    edge = send_lists.shape[3]
    taps_in = weight_one.shape[0]
    factor = 1.0 / math.sqrt(dp_size * slab_size * blocks * 64)
    voxels = blocks * 64
    slots = blocks + 2 * edge + 1
    packed = slab_size if (dp_size, slab_size, channels) == (4, 8, 256) else 0

    def array(*shape, dtype=BF16):
        return jax.ShapeDtypeStruct(shape, dtype)

    if packed:
        shares = [array(16, taps_in // slab_size // 2, 128)] * 2
    else:
        shares = [array(taps_in, channels, dtype=F32)]
    edges = array(edge, ROWS, 2 * channels)
    planes = pltpu.VMEM((4, slots, ROWS, channels), BF16)
    ends = pltpu.VMEM((2, slots, ROWS, channels), BF16)
    inner_shape = array(9, 4 * blocks * ROWS, channels)
    outer_shape = array(9, 2 * blocks * ROWS, channels)
    total = array(voxels, channels, dtype=F32)
    full = pltpu.VMEM((taps_in, channels) if packed else (8, channels), F32)
    sem = pltpu.SemaphoreType.DMA
    field = array(4, blocks, ROWS, channels)
    held = array(taps_in, channels)

    def scratch(shape):
        return pltpu.VMEM(shape.shape, shape.dtype)

    product = 2 * voxels * taps_in * channels
    around = array(4, slots, ROWS, channels)
    first, second, shift, source, source_other = call(
        pack_kernel,
        [edges, edges, array(8 * ROWS, 9 * ROWS), around, around],
        (send_lists, features, cotangent),
        "shh",
        [sem((2, 4))],
        limit=6,
    )
    got_first, got_second = swap_halos(first, second)
    inner, inner_other, before = call(
        inner_kernel,
        [inner_shape, inner_shape, total],
        (neighbour_table, source, source_other, shift, weight_one),
        "svvvh",
        [scratch(held), sem],
        limit=INNER_LIMIT,
        flops=2 * product,
    )
    hidden, outer, outer_other, *shares_two = call(
        functools.partial(forward_kernel, packed, ORDERS_TWO),
        [field, outer_shape, outer_shape] + shares,
        (
            neighbour_table,
            source,
            source_other,
            got_first,
            got_second,
            shift,
            weight_one,
            inner,
            inner_other,
            before,
        ),
        "svvvvvhvvv",
        [ends, full, scratch(held), sem],
        limit=FORWARD_LIMIT,
        flops=2 * product,
    )
    grad_hidden, first, second = call(
        middle_kernel,
        [field, edges, edges],
        (send_lists, inner_other, outer_other, weight_two, hidden),
        "svvvv",
        [scratch(total)],
        limit=4,
        flops=product,
    )
    shares_one = call(
        functools.partial(backward_kernel, packed, ORDERS_ONE),
        shares,
        (inner, outer, grad_hidden),
        "vvv",
        [full],
        limit=10,
        flops=product,
    )
    seconds = (
        (hidden, weight_two, features),
        (grad_hidden, weight_one, cotangent),
    )

    def finish(part, tokens, halos):
        got_first, got_second = halos
        source, weight, rows = seconds[part]
        (out,) = call(
            functools.partial(second_kernel, part, part == 1, len(tokens)),
            [array(*features.shape)],
            (
                neighbour_table,
                block_counts,
                source,
                got_first,
                got_second,
                shift,
                weight,
                rows,
                *tokens,
            ),
            "ssvvvvva" + "a" * len(tokens),
            [
                planes,
                pltpu.VMEM((blocks, 64, channels), BF16),
                scratch(inner_shape),
                scratch(outer_shape),
                scratch(total),
                sem,
            ],
            limit=10,
            flops=SECOND_COST * product,
        )
        return out

    if packed:
        terms, (output, grad_features) = reduce_packed(
            shares_one, shares_two, (first, second), finish
        )
        out = array(channels // dp_size, taps_in // slab_size, dtype=F32)
        grad_one, grad_two = (
            turned.T
            for turned in call(
                functools.partial(unpack_kernel, factor), [out, out], terms, "v" * len(terms)
            )
        )
    else:
        halos = swap_halos(first, second)
        output, grad_features = finish(0, [], halos), finish(1, [], halos)
        grad_one, grad_two = (
            lax.psum_scatter(
                lax.psum_scatter(share, "slab", scatter_dimension=0, tiled=True),
                "dp",
                scatter_dimension=1,
                tiled=True,
            )
            * factor
            for (share,) in (shares_one, shares_two)
        )
    return (output, grad_features, grad_one, grad_two)


def solution(mesh):
    in_specs = (
        P("dp", "slab", None, None),
        P("dp", "slab", None, None),
        P("dp", "slab", None),
        P("dp", "slab", None, None),
        P("dp", "slab"),
        P(),
        P(),
    )
    out_specs = (
        P("dp", "slab", None, None),
        P("dp", "slab", None, None),
        P("slab", "dp"),
        P("slab", "dp"),
    )
    return jax.shard_map(
        per_device, mesh=mesh, in_specs=in_specs, out_specs=out_specs, check_vma=False
    )
```

profile of v0, /device:TPU:0, one launch (start us, length us, event | category | flops | bytes accessed | tf_op | source)
XLA Modules:
  0.0 80.4 jit_solution(10979134203754772505)
XLA Ops:
  0.6 1.0 %copy-done = bf16[1,10,64,256]{3,2,1,0:T(8,128)(2,1)S(1)} copy-done((bf16[1,10,64,256]{3,2,1,0:T(8,128)(2,1)S(1)}, bf16[1,10,64,256]{3,2,1,0:T(8,128)(2,1)}, u32[]{:S(2)}) %copy-start) | copy-done | bytes 327704
  1.6 1.0 %copy-done.2 = bf16[1,10,64,256]{3,2,1,0:T(8,128)(2,1)S(1)} copy-done((bf16[1,10,64,256]{3,2,1,0:T(8,128)(2,1)S(1)}, bf16[1,10,64,256]{3,2,1,0:T(8,128)(2,1)}, u32[]{:S(2)}) %copy-start.2) | copy-done | bytes 327704
  2.6 0.7 copy-done.4
  3.3 0.8 %shard_map.102 = (bf16[2,16,512]{2,1,0:T(8,128)(2,1)S(1)}, bf16[2,16,512]{2,1,0:T(8,128)(2,1)S(1)}, bf16[128,144]{1,0:T(8,128)(2,1)S(1)}, bf16[4,15,16,256]{3,2,...) custom-call(s32[1,1,2,2]{3,2,1,0:T(2,128)S(1)} %copy-done.4, bf16[1,10,64,256]{3,2,1,0:T(8,128)(2,1)S(1)} %copy-done, ...), custom_call_target="tpu_custom_call" | custom-call | tf_op jit(solution)/shard_map/pallas_call | solution.py:357
  4.1 3.0 %collective-permute-start = (bf16[2,16,512]{2,1,0:T(8,128)(2,1)S(1)}, bf16[2,16,512]{2,1,0:T(8,128)(2,1)S(1)}, u32[]{:S(2)}, u32[]{:S(2)}) collective-permute-start(bf16[2,16,512]{2,1,0:T(8,128)(2,1)S(1)} %get-tuple-element.47), channel_id=1, source_target_pairs={{0,1},{1,0},{2,3},{3,2},{4,5},{5,4},{6,7},{7,6},{8,9},{9,8},{10,11... | collective-permute-start | bytes 98312 | tf_op jit(solution)/shard_map/ppermute | solution.py:75
  7.1 0.7 collective-permute-start.1
  7.8 0.7 copy.12.table
  8.5 5.1 %shard_map.103 = (bf16[9,640,256]{2,1,0:T(8,128)(2,1)S(1)}, bf16[9,640,256]{2,1,0:T(8,128)(2,1)S(1)}, f32[640,256]{1,0:T(8,128)S(1)}) custom-call(s32[1,10,27]{2,1,0:T(8,128)S(1)} %copy.12.table, bf16[4,15,16,256]{3,2,1,0:T(8,128)(2,1)S(1)} %get-tuple-element.45.planes.source, bf16[4,15,16,256]{3,2,1,0:T(8,128)(2,1)S(1)} %get-tuple-element.46.more.source_other, ...), custom_call_target="tpu_custom_call" | custom-call | flops 4529848320 | tf_op jit(solution)/shard_map/pallas_call | solution.py:357
  13.6 6.4 %shard_map.104 = (bf16[4,10,16,256]{3,2,1,0:T(8,128)(2,1)S(1)}, bf16[9,320,256]{2,1,0:T(8,128)(2,1)S(1)}, bf16[9,320,256]{2,1,0:T(8,128)(2,1)S(1)}, bf16[16,432,...) custom-call(s32[1,10,27]{2,1,0:T(8,128)S(1)} %copy.12.table, bf16[4,15,16,256]{3,2,1,0:T(8,128)(2,1)S(1)} %get-tuple-element.45.planes.source, ...), custom_call_target="tpu_custom_call" | custom-call | flops 4529848320 | tf_op jit(solution)/shard_map/pallas_call | solution.py:357
  20.2 3.0 %shard_map.105 = (bf16[4,10,16,256]{3,2,1,0:T(8,128)(2,1)S(1)}, bf16[2,16,512]{2,1,0:T(8,128)(2,1)S(1)}, bf16[2,16,512]{2,1,0:T(8,128)(2,1)S(1)}) custom-call(s32[1,1,2,2]{3,2,1,0:T(2,128)S(1)} %copy-done.5, bf16[9,640,256]{2,1,0:T(8,128)(2,1)S(1)} %get-tuple-element.51.other.inner, bf16[9,320,256]{2,1,0:T(8,128)(2,1)S(1)} %get-tuple-element.56.outer, ...), custom_call_target="tpu_custom_call" | custom-call | flops 2264924160 | tf_op jit(solution)/shard_map/pallas_call | solution.py:357
  23.2 3.5 %shard_map.106 = (bf16[16,432,128]{2,1,0:T(8,128)(2,1)S(1)}, bf16[16,432,128]{2,1,0:T(8,128)(2,1)S(1)}) custom-call(bf16[9,640,256]{2,1,0:T(8,128)(2,1)S(1)} %get-tuple-element.50.inner, bf16[9,320,256]{2,1,0:T(8,128)(2,1)S(1)} %get-tuple-element.59.outer, bf16[4,10,16,256]{3,2,1,0:T(8,128)(2,1)S(1)} %get-tuple-element.60.grad_hidden.source), custom_call_target="tpu_custom_call" | custom-call | flops 2264924160 | tf_op jit(solution)/shard_map/pallas_call | solution.py:357
  26.7 0.5 collective-permute-start.5
  28.1 4.3 %collective-permute-start.3 = (bf16[2,16,512]{2,1,0:T(8,128)(2,1)S(1)}, bf16[2,16,512]{2,1,0:T(8,128)(2,1)S(1)}, u32[]{:S(2)}, u32[]{:S(2)}) collective-permute-start(bf16[2,16,512]{2,1,0:T(8,128)(2,1)S(1)} %get-tuple-element.57), channel_id=1, source_target_pairs={{0,1},{1,0},{2,3},{3,2},{4,5},{5,4},{6,7},{7,6},{8,9},{9,8},{10,11... | collective-permute-start | bytes 98312 | tf_op jit(solution)/shard_map/ppermute | solution.py:75
  32.4 0.8 %collective-permute-start.4 = (bf16[2,16,512]{2,1,0:T(8,128)(2,1)S(1)}, bf16[2,16,512]{2,1,0:T(8,128)(2,1)S(1)}, u32[]{:S(2)}, u32[]{:S(2)}) collective-permute-start(bf16[2,16,512]{2,1,0:T(8,128)(2,1)S(1)} %get-tuple-element.58), channel_id=1, source_target_pairs={{1,2},{2,1},{3,4},{4,3},{5,6},{6,5},{9,10},{10,9},{11,12},{12,11},... | collective-permute-start | bytes 98312 | tf_op jit(solution)/shard_map/ppermute | solution.py:75
  33.9 1.6 %collective-permute-start.7 = (bf16[8,176,128]{2,1,0:T(8,128)(2,1)S(1)}, bf16[8,176,128]{2,1,0:T(8,128)(2,1)S(1)}, u32[]{:S(2)}, u32[]{:S(2)}) collective-permute-start(bf16[8,176,128]{2,1,0:T(8,128)(2,1)S(1)} %get-tuple-element.69), channel_id=1, source_target_pairs={{0,16},{1,17},{2,18},{3,19},{4,20},{5,21},{6,22},{7,23},{8,24},{9,... | collective-permute-start | bytes 1081352 | tf_op jit(solution)/shard_map/ppermute | solution.py:68
  35.5 2.8 %collective-permute-start.6 = (bf16[8,256,128]{2,1,0:T(8,128)(2,1)S(1)}, bf16[8,256,128]{2,1,0:T(8,128)(2,1)S(1)}, u32[]{:S(2)}, u32[]{:S(2)}) collective-permute-start(bf16[8,256,128]{2,1,0:T(8,128)(2,1)S(1)} %get-tuple-element.67), channel_id=1, source_target_pairs={{0,2},{1,3},{2,0},{3,1},{4,6},{5,7},{6,4},{7,5},{8,10},{9,11},{10,... | collective-permute-start | bytes 1572872 | tf_op jit(solution)/shard_map/ppermute | solution.py:68
  38.4 0.6 collective-permute-start.9
  39.0 3.0 %collective-permute-start.8 = (bf16[8,288,128]{2,1,0:T(8,128)(2,1)S(1)}, bf16[8,288,128]{2,1,0:T(8,128)(2,1)S(1)}, u32[]{:S(2)}, u32[]{:S(2)}) collective-permute-start(bf16[8,288,128]{2,1,0:T(8,128)(2,1)S(1)} %get-tuple-element.87.rest_0_), channel_id=1, source_target_pairs={{0,1},{1,0},{2,3},{3,2},{4,5},{5,4},{6,7},{7,6},{8,9},{9,8},{10,11... | collective-permute-start | bytes 1769480 | tf_op jit(solution)/shard_map/ppermute | solution.py:68
  42.0 5.8 %shard_map.107 = bf16[1,10,64,256]{3,2,1,0:T(8,128)(2,1)} custom-call(s32[1,10,27]{2,1,0:T(8,128)S(1)} %copy.12.table, s32[1,1]{1,0:T(1,128)S(6)} %copy.15.counts, bf16[4,10,16,256]{3,2,1,0:T(8,128)(2,1)S(1)} %get-tuple-element.55.hidden.source, bf16[2,16,512]{2,1,0:T(8,128)(2,1)S(1)} %collective-permute-done.3.got_first, ...), custom_call_target="tpu_custom_call" | custom-call | flops 2264924160 | tf_op jit(solution)/shard_map/pallas_call | solution.py:357
  47.9 1.9 %collective-permute-done.6 = bf16[8,256,128]{2,1,0:T(8,128)(2,1)S(1)} collective-permute-done((bf16[8,256,128]{2,1,0:T(8,128)(2,1)S(1)}, bf16[8,256,128]{2,1,0:T(8,128)(2,1)S(1)}, u32[]{:S(2)}, u32[]{:S(2)}) %collective-permute-start.6) | collective-permute-done | bytes 524320 | tf_op jit(solution)/shard_map/ppermute | solution.py:68
  50.1 0.7 collective-permute-start.10
  50.8 1.6 %collective-permute-start.11 = (bf16[4,176,128]{2,1,0:T(8,128)(2,1)S(1)}, bf16[4,176,128]{2,1,0:T(8,128)(2,1)S(1)}, u32[]{:S(2)}, u32[]{:S(2)}) collective-permute-start(bf16[4,176,128]{2,1,0:T(8,128)(2,1)S(1)} %get-tuple-element.76), channel_id=1, source_target_pairs={{0,2},{1,3},{2,0},{3,1},{4,6},{5,7},{6,4},{7,5},{8,10},{9,11},{10,... | collective-permute-start | bytes 540680 | tf_op jit(solution)/shard_map/ppermute | solution.py:68
  52.5 2.8 %collective-permute-start.13 = (bf16[4,144,128]{2,1,0:T(8,128)(2,1)S(1)}, bf16[4,144,128]{2,1,0:T(8,128)(2,1)S(1)}, u32[]{:S(2)}, u32[]{:S(2)}) collective-permute-start(bf16[4,144,128]{2,1,0:T(8,128)(2,1)S(1)} %get-tuple-element.105.rest_1_), channel_id=1, source_target_pairs={{0,1},{1,0},{2,3},{3,2},{4,5},{5,4},{6,7},{7,6},{8,9},{9,8},{10,11... | collective-permute-start | bytes 442376 | tf_op jit(solution)/shard_map/ppermute | solution.py:68
  55.5 2.2 %collective-permute-start.12 = (bf16[4,288,128]{2,1,0:T(8,128)(2,1)S(1)}, bf16[4,288,128]{2,1,0:T(8,128)(2,1)S(1)}, u32[]{:S(2)}, u32[]{:S(2)}) collective-permute-start(bf16[4,288,128]{2,1,0:T(8,128)(2,1)S(1)} %get-tuple-element.93.rest_0_), channel_id=1, source_target_pairs={{0,16},{1,17},{2,18},{3,19},{4,20},{5,21},{6,22},{7,23},{8,24},{9,... | collective-permute-start | bytes 884744 | tf_op jit(solution)/shard_map/ppermute | solution.py:68
  57.8 5.8 %shard_map.108 = bf16[1,10,64,256]{3,2,1,0:T(8,128)(2,1)} custom-call(s32[1,10,27]{2,1,0:T(8,128)S(1)} %copy.12.table, s32[1,1]{1,0:T(1,128)S(6)} %copy.15.counts, bf16[4,10,16,256]{3,2,1,0:T(8,128)(2,1)S(1)} %get-tuple-element.60.grad_hidden.source, bf16[2,16,512]{2,1,0:T(8,128)(2,1)S(1)} %collective-permute-done.3.got_first, ...), custom_call_target="tpu_custom_call" | custom-call | flops 2264924160 | tf_op jit(solution)/shard_map/pallas_call | solution.py:357
  64.0 1.6 %collective-permute-start.15 = (bf16[2,432,128]{2,1,0:T(8,128)(2,1)S(1)}, bf16[2,432,128]{2,1,0:T(8,128)(2,1)S(1)}, u32[]{:S(2)}, u32[]{:S(2)}) collective-permute-start(bf16[2,432,128]{2,1,0:T(8,128)(2,1)S(1)} %get-tuple-element.82), channel_id=1, source_target_pairs={{0,2},{1,3},{2,0},{3,1},{4,6},{5,7},{6,4},{7,5},{8,10},{9,11},{10,... | collective-permute-start | bytes 663560 | tf_op jit(solution)/shard_map/ppermute | solution.py:68
  65.6 4.1 %collective-permute-done.14 = bf16[2,432,128]{2,1,0:T(8,128)(2,1)S(1)} collective-permute-done((bf16[2,432,128]{2,1,0:T(8,128)(2,1)S(1)}, bf16[2,432,128]{2,1,0:T(8,128)(2,1)S(1)}, u32[]{:S(2)}, u32[]{:S(2)}) %collective-permute-start.14) | collective-permute-done | bytes 221216 | tf_op jit(solution)/shard_map/ppermute | solution.py:68
  69.9 2.2 %collective-permute-done.15 = bf16[2,432,128]{2,1,0:T(8,128)(2,1)S(1)} collective-permute-done((bf16[2,432,128]{2,1,0:T(8,128)(2,1)S(1)}, bf16[2,432,128]{2,1,0:T(8,128)(2,1)S(1)}, u32[]{:S(2)}, u32[]{:S(2)}) %collective-permute-start.15) | collective-permute-done | bytes 221216 | tf_op jit(solution)/shard_map/ppermute | solution.py:68
  72.1 2.3 %collective-permute-start.16 = (bf16[1,432,128]{2,1,0:T(8,128)(2,1)S(1)}, bf16[1,432,128]{2,1,0:T(8,128)(2,1)S(1)}, u32[]{:S(2)}, u32[]{:S(2)}) collective-permute-start(bf16[1,432,128]{2,1,0:T(8,128)(2,1)S(1)} %get-tuple-element.108), channel_id=1, source_target_pairs={{0,4},{1,5},{2,6},{3,7},{4,0},{5,1},{6,2},{7,3},{8,12},{9,13},{10,... | collective-permute-start | bytes 331784 | tf_op jit(solution)/shard_map/ppermute | solution.py:68
  74.5 2.3 %collective-permute-done.17 = bf16[1,432,128]{2,1,0:T(8,128)(2,1)S(1)} collective-permute-done((bf16[1,432,128]{2,1,0:T(8,128)(2,1)S(1)}, bf16[1,432,128]{2,1,0:T(8,128)(2,1)S(1)}, u32[]{:S(2)}, u32[]{:S(2)}) %collective-permute-start.17) | collective-permute-done | bytes 110624 | tf_op jit(solution)/shard_map/ppermute | solution.py:68
  76.7 2.4 %collective-permute-done.16 = bf16[1,432,128]{2,1,0:T(8,128)(2,1)S(1)} collective-permute-done((bf16[1,432,128]{2,1,0:T(8,128)(2,1)S(1)}, bf16[1,432,128]{2,1,0:T(8,128)(2,1)S(1)}, u32[]{:S(2)}, u32[]{:S(2)}) %collective-permute-start.16) | collective-permute-done | bytes 110624 | tf_op jit(solution)/shard_map/ppermute | solution.py:68
  79.1 1.3 %shard_map.109 = (f32[64,864]{1,0:T(8,128)}, f32[64,864]{1,0:T(8,128)}) custom-call(bf16[432,128]{1,0:T(8,128)(2,1)S(1)} %get-tuple-element.109.refs_0_, bf16[432,128]{1,0:T(8,128)(2,1)S(1)} %bitcast.9, bf16[432,128]{1,0:T(8,128)(2,1)S(1)} %get-tuple-element.106.refs_2_, bf16[432,128]{1,0:T(8,128)(2,1)S(1)} %bitcast.8), custom_call_target="tpu_custom_call" | custom-call | tf_op jit(solution)/shard_map/pallas_call | solution.py:357
  (55 shorter events, 2.2 us)
Async XLA Ops:
  0.6 1.0 %copy-start = (bf16[1,10,64,256]{3,2,1,0:T(8,128)(2,1)S(1)}, bf16[1,10,64,256]{3,2,1,0:T(8,128)(2,1)}, u32[]{:S(2)}) copy-start(bf16[1,10,64,256]{3,2,1,0:T(8,128)(2,1)} %rows.2) | copy-start | bytes 983044
  1.6 1.0 %copy-start.2 = (bf16[1,10,64,256]{3,2,1,0:T(8,128)(2,1)S(1)}, bf16[1,10,64,256]{3,2,1,0:T(8,128)(2,1)}, u32[]{:S(2)}) copy-start(bf16[1,10,64,256]{3,2,1,0:T(8,128)(2,1)} %rows.3) | copy-start | bytes 983044
  2.6 0.7 copy-start.4
  4.1 9.5 %collective-permute-start = (bf16[2,16,512]{2,1,0:T(8,128)(2,1)S(1)}, bf16[2,16,512]{2,1,0:T(8,128)(2,1)S(1)}, u32[]{:S(2)}, u32[]{:S(2)}) collective-permute-start(bf16[2,16,512]{2,1,0:T(8,128)(2,1)S(1)} %get-tuple-element.47), channel_id=1, source_target_pairs={{0,1},{1,0},{2,3},{3,2},{4,5},{5,4},{6,7},{7,6},{8,9},{9,8},{10,11... | collective-permute-start | bytes 98312 | tf_op jit(solution)/shard_map/ppermute | solution.py:75
  7.1 6.5 %collective-permute-start.1 = (bf16[2,16,512]{2,1,0:T(8,128)(2,1)S(1)}, bf16[2,16,512]{2,1,0:T(8,128)(2,1)S(1)}, u32[]{:S(2)}, u32[]{:S(2)}) collective-permute-start(bf16[2,16,512]{2,1,0:T(8,128)(2,1)S(1)} %get-tuple-element.48), channel_id=1, source_target_pairs={{1,2},{2,1},{3,4},{4,3},{5,6},{6,5},{9,10},{10,9},{11,12},{12,11},... | collective-permute-start | bytes 98312 | tf_op jit(solution)/shard_map/ppermute | solution.py:75
  8.5 5.1 %copy-start.7 = (bf16[6912,256]{1,0:T(8,128)(2,1)S(1)}, bf16[6912,256]{1,0:T(8,128)(2,1)}, u32[]{:S(2)}) copy-start(bf16[6912,256]{1,0:T(8,128)(2,1)} %weight.9) | copy-start | bytes 10616836
  13.6 6.6 %copy-start.5 = (s32[1,1,2,2]{3,2,1,0:T(2,128)S(1)}, s32[1,1,2,2]{3,2,1,0:T(2,128)}, u32[]{:S(2)}) copy-start(s32[1,1,2,2]{3,2,1,0:T(2,128)} %lists.3) | copy-start | bytes 52
  13.6 6.6 %copy-start.6 = (bf16[6912,256]{1,0:T(8,128)(2,1)S(1)}, bf16[6912,256]{1,0:T(8,128)(2,1)}, u32[]{:S(2)}) copy-start(bf16[6912,256]{1,0:T(8,128)(2,1)} %weight.8) | copy-start | bytes 10616836
  20.1 13.2 %collective-permute-start.2 = (bf16[16,432,128]{2,1,0:T(8,128)(2,1)S(1)}, bf16[16,432,128]{2,1,0:T(8,128)(2,1)S(1)}, u32[]{:S(2)}, u32[]{:S(2)}) collective-permute-start(bf16[16,432,128]{2,1,0:T(8,128)(2,1)S(1)} %get-tuple-element.54), channel_id=1, source_target_pairs={{0,8},{1,9},{2,10},{3,11},{4,12},{5,13},{6,14},{7,15},{8,0},{9,1},... | collective-permute-start | bytes 5308424 | tf_op jit(solution)/shard_map/ppermute | solution.py:68
  26.7 6.9 %collective-permute-start.5 = (bf16[16,432,128]{2,1,0:T(8,128)(2,1)S(1)}, bf16[16,432,128]{2,1,0:T(8,128)(2,1)S(1)}, u32[]{:S(2)}, u32[]{:S(2)}) collective-permute-start(bf16[16,432,128]{2,1,0:T(8,128)(2,1)S(1)} %get-tuple-element.63), channel_id=1, source_target_pairs={{0,8},{1,9},{2,10},{3,11},{4,12},{5,13},{6,14},{7,15},{8,0},{9,1},... | collective-permute-start | bytes 5308424 | tf_op jit(solution)/shard_map/ppermute | solution.py:68
  28.1 10.9 %collective-permute-start.3 = (bf16[2,16,512]{2,1,0:T(8,128)(2,1)S(1)}, bf16[2,16,512]{2,1,0:T(8,128)(2,1)S(1)}, u32[]{:S(2)}, u32[]{:S(2)}) collective-permute-start(bf16[2,16,512]{2,1,0:T(8,128)(2,1)S(1)} %get-tuple-element.57), channel_id=1, source_target_pairs={{0,1},{1,0},{2,3},{3,2},{4,5},{5,4},{6,7},{7,6},{8,9},{9,8},{10,11... | collective-permute-start | bytes 98312 | tf_op jit(solution)/shard_map/ppermute | solution.py:75
  32.4 9.6 %collective-permute-start.4 = (bf16[2,16,512]{2,1,0:T(8,128)(2,1)S(1)}, bf16[2,16,512]{2,1,0:T(8,128)(2,1)S(1)}, u32[]{:S(2)}, u32[]{:S(2)}) collective-permute-start(bf16[2,16,512]{2,1,0:T(8,128)(2,1)S(1)} %get-tuple-element.58), channel_id=1, source_target_pairs={{1,2},{2,1},{3,4},{4,3},{5,6},{6,5},{9,10},{10,9},{11,12},{12,11},... | collective-permute-start | bytes 98312 | tf_op jit(solution)/shard_map/ppermute | solution.py:75
  33.9 8.1 %copy-start.1 = (bf16[1,10,64,256]{3,2,1,0:T(8,128)(2,1)S(1)}, bf16[1,10,64,256]{3,2,1,0:T(8,128)(2,1)}, u32[]{:S(2)}) copy-start(bf16[1,10,64,256]{3,2,1,0:T(8,128)(2,1)} %rows.2) | copy-start | bytes 983044
  33.9 13.9 %collective-permute-start.7 = (bf16[8,176,128]{2,1,0:T(8,128)(2,1)S(1)}, bf16[8,176,128]{2,1,0:T(8,128)(2,1)S(1)}, u32[]{:S(2)}, u32[]{:S(2)}) collective-permute-start(bf16[8,176,128]{2,1,0:T(8,128)(2,1)S(1)} %get-tuple-element.69), channel_id=1, source_target_pairs={{0,16},{1,17},{2,18},{3,19},{4,20},{5,21},{6,22},{7,23},{8,24},{9,... | collective-permute-start | bytes 1081352 | tf_op jit(solution)/shard_map/ppermute | solution.py:68
  35.5 14.4 %collective-permute-start.6 = (bf16[8,256,128]{2,1,0:T(8,128)(2,1)S(1)}, bf16[8,256,128]{2,1,0:T(8,128)(2,1)S(1)}, u32[]{:S(2)}, u32[]{:S(2)}) collective-permute-start(bf16[8,256,128]{2,1,0:T(8,128)(2,1)S(1)} %get-tuple-element.67), channel_id=1, source_target_pairs={{0,2},{1,3},{2,0},{3,1},{4,6},{5,7},{6,4},{7,5},{8,10},{9,11},{10,... | collective-permute-start | bytes 1572872 | tf_op jit(solution)/shard_map/ppermute | solution.py:68
  38.4 13.9 %collective-permute-start.9 = (bf16[8,144,128]{2,1,0:T(8,128)(2,1)S(1)}, bf16[8,144,128]{2,1,0:T(8,128)(2,1)S(1)}, u32[]{:S(2)}, u32[]{:S(2)}) collective-permute-start(bf16[8,144,128]{2,1,0:T(8,128)(2,1)S(1)} %get-tuple-element.95.rest_1_), channel_id=1, source_target_pairs={{0,16},{1,17},{2,18},{3,19},{4,20},{5,21},{6,22},{7,23},{8,24},{9,... | collective-permute-start | bytes 884744 | tf_op jit(solution)/shard_map/ppermute | solution.py:68
  39.0 16.3 %collective-permute-start.8 = (bf16[8,288,128]{2,1,0:T(8,128)(2,1)S(1)}, bf16[8,288,128]{2,1,0:T(8,128)(2,1)S(1)}, u32[]{:S(2)}, u32[]{:S(2)}) collective-permute-start(bf16[8,288,128]{2,1,0:T(8,128)(2,1)S(1)} %get-tuple-element.87.rest_0_), channel_id=1, source_target_pairs={{0,1},{1,0},{2,3},{3,2},{4,5},{5,4},{6,7},{7,6},{8,9},{9,8},{10,11... | collective-permute-start | bytes 1769480 | tf_op jit(solution)/shard_map/ppermute | solution.py:68
  50.1 13.5 %collective-permute-start.10 = (bf16[4,256,128]{2,1,0:T(8,128)(2,1)S(1)}, bf16[4,256,128]{2,1,0:T(8,128)(2,1)S(1)}, u32[]{:S(2)}, u32[]{:S(2)}) collective-permute-start(bf16[4,256,128]{2,1,0:T(8,128)(2,1)S(1)} %get-tuple-element.75), channel_id=1, source_target_pairs={{0,16},{1,17},{2,18},{3,19},{4,20},{5,21},{6,22},{7,23},{8,24},{9,... | collective-permute-start | bytes 786440 | tf_op jit(solution)/shard_map/ppermute | solution.py:68
  50.8 12.8 %collective-permute-start.11 = (bf16[4,176,128]{2,1,0:T(8,128)(2,1)S(1)}, bf16[4,176,128]{2,1,0:T(8,128)(2,1)S(1)}, u32[]{:S(2)}, u32[]{:S(2)}) collective-permute-start(bf16[4,176,128]{2,1,0:T(8,128)(2,1)S(1)} %get-tuple-element.76), channel_id=1, source_target_pairs={{0,2},{1,3},{2,0},{3,1},{4,6},{5,7},{6,4},{7,5},{8,10},{9,11},{10,... | collective-permute-start | bytes 540680 | tf_op jit(solution)/shard_map/ppermute | solution.py:68
  52.5 5.3 %copy-start.3 = (bf16[1,10,64,256]{3,2,1,0:T(8,128)(2,1)S(1)}, bf16[1,10,64,256]{3,2,1,0:T(8,128)(2,1)}, u32[]{:S(2)}) copy-start(bf16[1,10,64,256]{3,2,1,0:T(8,128)(2,1)} %rows.3) | copy-start | bytes 983044
  52.5 11.3 %collective-permute-start.13 = (bf16[4,144,128]{2,1,0:T(8,128)(2,1)S(1)}, bf16[4,144,128]{2,1,0:T(8,128)(2,1)S(1)}, u32[]{:S(2)}, u32[]{:S(2)}) collective-permute-start(bf16[4,144,128]{2,1,0:T(8,128)(2,1)S(1)} %get-tuple-element.105.rest_1_), channel_id=1, source_target_pairs={{0,1},{1,0},{2,3},{3,2},{4,5},{5,4},{6,7},{7,6},{8,9},{9,8},{10,11... | collective-permute-start | bytes 442376 | tf_op jit(solution)/shard_map/ppermute | solution.py:68
  55.5 8.3 %collective-permute-start.12 = (bf16[4,288,128]{2,1,0:T(8,128)(2,1)S(1)}, bf16[4,288,128]{2,1,0:T(8,128)(2,1)S(1)}, u32[]{:S(2)}, u32[]{:S(2)}) collective-permute-start(bf16[4,288,128]{2,1,0:T(8,128)(2,1)S(1)} %get-tuple-element.93.rest_0_), channel_id=1, source_target_pairs={{0,16},{1,17},{2,18},{3,19},{4,20},{5,21},{6,22},{7,23},{8,24},{9,... | collective-permute-start | bytes 884744 | tf_op jit(solution)/shard_map/ppermute | solution.py:68
  63.7 6.0 %collective-permute-start.14 = (bf16[2,432,128]{2,1,0:T(8,128)(2,1)S(1)}, bf16[2,432,128]{2,1,0:T(8,128)(2,1)S(1)}, u32[]{:S(2)}, u32[]{:S(2)}) collective-permute-start(bf16[2,432,128]{2,1,0:T(8,128)(2,1)S(1)} %get-tuple-element.80), channel_id=1, source_target_pairs={{0,1},{1,0},{2,3},{3,2},{4,5},{5,4},{6,7},{7,6},{8,9},{9,8},{10,11... | collective-permute-start | bytes 663560 | tf_op jit(solution)/shard_map/ppermute | solution.py:68
  64.0 8.1 %collective-permute-start.15 = (bf16[2,432,128]{2,1,0:T(8,128)(2,1)S(1)}, bf16[2,432,128]{2,1,0:T(8,128)(2,1)S(1)}, u32[]{:S(2)}, u32[]{:S(2)}) collective-permute-start(bf16[2,432,128]{2,1,0:T(8,128)(2,1)S(1)} %get-tuple-element.82), channel_id=1, source_target_pairs={{0,2},{1,3},{2,0},{3,1},{4,6},{5,7},{6,4},{7,5},{8,10},{9,11},{10,... | collective-permute-start | bytes 663560 | tf_op jit(solution)/shard_map/ppermute | solution.py:68
  69.8 6.9 %collective-permute-start.17 = (bf16[1,432,128]{2,1,0:T(8,128)(2,1)S(1)}, bf16[1,432,128]{2,1,0:T(8,128)(2,1)S(1)}, u32[]{:S(2)}, u32[]{:S(2)}) collective-permute-start(bf16[1,432,128]{2,1,0:T(8,128)(2,1)S(1)} %get-tuple-element.83), channel_id=1, source_target_pairs={{0,4},{1,5},{2,6},{3,7},{4,0},{5,1},{6,2},{7,3},{8,12},{9,13},{10,... | collective-permute-start | bytes 331784 | tf_op jit(solution)/shard_map/ppermute | solution.py:68
  72.1 6.9 %collective-permute-start.16 = (bf16[1,432,128]{2,1,0:T(8,128)(2,1)S(1)}, bf16[1,432,128]{2,1,0:T(8,128)(2,1)S(1)}, u32[]{:S(2)}, u32[]{:S(2)}) collective-permute-start(bf16[1,432,128]{2,1,0:T(8,128)(2,1)S(1)} %get-tuple-element.108), channel_id=1, source_target_pairs={{0,4},{1,5},{2,6},{3,7},{4,0},{5,1},{6,2},{7,3},{8,12},{9,13},{10,... | collective-permute-start | bytes 331784 | tf_op jit(solution)/shard_map/ppermute | solution.py:68
where the time goes:
time: 80.7 us; the launch traced here: 80.4 us
  Pallas kernels  31.8 us (39%)
  starting transfers between devices  28.9 us (36%)
  waiting for transfers between devices  12.9 us (16%)
  local copies, waits for them, and re-layouts  3.94 us (5%)
  between operations  1.67 us (2%)
  other arithmetic  1.26 us (2%)
    pallas_call x8, Pallas kernels, call(): pl.pallas_call(kernel, out_shape=outs, in_specs=[pl.BlockSpec(memory_spac...  31.8 us
    ppermute x14, starting transfers between devices, swap(): lax.ppermute(array, ('dp', 'slab'), pair_perm(name, dp_size, slab_size))  20 us
    ppermute x14, waiting for transfers between devices, swap(): lax.ppermute(array, ('dp', 'slab'), pair_perm(name, dp_size, slab_size))  12.9 us
    ppermute x2, starting transfers between devices, swap_halos(): lax.ppermute(first, 'slab', even)  7.35 us
    unnamed x17, local copies, waits for them, and re-layouts  3.34 us
  transfers between devices with their start and end apart: 18, of which 5 were waited for; matrix products, arithmetic and copies ran while one was open for 3% of the time, Pallas kernels for 29%

commit v1 on v0

--- a/solution.py
+++ b/solution.py
@@ -14,33 +14,33 @@
 ROWS = 16
 MIB = 2**20
 SECOND_COST = 1
-INNER_LIMIT = 44
+INNER_LIMIT = 42
 FORWARD_LIMIT = 14
 UNROLL = 5
 
 ORDERS_ONE = (
-    (0, 288, ("x", "y", "z1")),
-    (288, 432, ("y", "x", "z1")),
+    (0, 288, ("z1", "y", "x")),
+    (288, 432, ("y", "z1", "x")),
 )
 ORDERS_TWO = (
-    (0, 256, ("z1", "y", "x")),
-    (256, 432, ("y", "z1", "x")),
+    (0, 256, ("x", "y", "z1")),
+    (256, 432, ("y", "x", "z1")),
 )
 LAST = "z2"
 
 
 def shift_matrix():
-    shape = (8 * ROWS, 9 * ROWS)
+    shape = (16 * ROWS, 12 * ROWS)
     row = lax.broadcasted_iota(jnp.int32, shape, 0)
     column = lax.broadcasted_iota(jnp.int32, shape, 1)
-    shift = row >> 4
+    shift = (row >> 4) & 7
     shift = jnp.where(shift >= 4, shift + 1, shift)
     across = jnp.where(shift >= 6, 2, jnp.where(shift >= 3, 1, 0))
     y = ((row >> 2) & 3) + across + 3
     z = (row & 3) + (shift - 3 * across) + 3
-    plane = 3 * (y >> 2) + (z >> 2)
-    source = 16 * plane + 4 * (y & 3) + (z & 3)
-    return jnp.where(column == source, 1.0, 0.0).astype(BF16)
+    own = jnp.where((y >> 2) == 1, 16, 0)
+    source = 32 * (z >> 2) + own + 4 * (y & 3) + (z & 3)
+    return jnp.where(column == source + 96 * (row >> 7), 1.0, 0.0).astype(BF16)
 
 
 def bit_of(name, dp_index, slab_index):
@@ -75,10 +75,10 @@
     return lax.ppermute(first, "slab", even), lax.ppermute(second, "slab", odd)
 
 
-def pack_kernel(lists, features, cotangent, first, second, shift, planes, more, sems):
-    blocks, channels = features.shape[1], features.shape[3]
-    copies = start_planes(planes, features, blocks, sems.at[0])
-    copies += start_planes(more, cotangent, blocks, sems.at[1])
+def pack_kernel(lists, fields, first, second, shift, planes, more, sems):
+    blocks = fields.shape[1]
+    copies = start_planes(planes, fields.at[0:1], blocks, sems.at[0])
+    copies += start_planes(more, fields.at[1:2], blocks, sems.at[1])
     shift[...] = shift_matrix()
     for field in (planes, more):
         field[:, blocks:] = jnp.zeros_like(field[:, blocks:])
@@ -125,19 +125,28 @@
 
 def gather_shifts(shifted, planes, table, shift, blocks, wanted):
     matrix = shift[...]
+    upper = lax.broadcasted_iota(jnp.int32, (ROWS, planes.shape[3]), 0) < 8
 
     def one_block(b, carry):
-        for place, (at, slab) in enumerate(wanted):
-            near_x = 0 if at == 0 else 2 if at == 5 else 1
-            around = [planes[slab, table[0, b, 9 * near_x + n]] for n in range(9)]
+        for place in range(0, len(wanted), 2):
+            stack, centres = [], []
+            for at, slab in wanted[place : place + 2]:
+                near_x = 0 if at == 0 else 2 if at == 5 else 1
+                around = [planes[slab, table[b, 0, 9 * near_x + n]] for n in range(9)]
+                for z in range(3):
+                    stack += [jnp.where(upper, around[6 + z], around[z]), around[3 + z]]
+                centres.append(around[4])
             moved = jnp.dot(
-                matrix, jnp.concatenate(around, axis=0), preferred_element_type=F32
+                matrix, jnp.concatenate(stack, axis=0), preferred_element_type=F32
             ).astype(BF16)
-            pieces = [moved[n * ROWS : (n + 1) * ROWS] for n in range(8)]
-            pieces.insert(4, around[4])
-            for n, piece in enumerate(pieces):
-                start = place * blocks * ROWS + b * ROWS
-                shifted[n, pl.ds(pl.multiple_of(start, ROWS), ROWS), :] = piece
+            for half in range(2):
+                pieces = [
+                    moved[(8 * half + n) * ROWS : (8 * half + n + 1) * ROWS] for n in range(8)
+                ]
+                pieces.insert(4, centres[half])
+                for n, piece in enumerate(pieces):
+                    start = (place + half) * blocks * ROWS + b * ROWS
+                    shifted[n, pl.ds(pl.multiple_of(start, ROWS), ROWS), :] = piece
         return carry
 
     lax.fori_loop(0, blocks, one_block, 0, unroll=UNROLL)
@@ -237,11 +246,16 @@
 
 def inner_kernel(table, planes, more, shift, weight, inner, other, before, held, sem):
     blocks = before.shape[0] // 64
-    fetch = pltpu.make_async_copy(weight, held, sem)
-    fetch.start()
+    third = weight.shape[0] // 3
+    fetches = []
+    for i in (1, 0, 2):
+        rows = pl.ds(i * third, third)
+        fetches.append(pltpu.make_async_copy(weight.at[rows], held.at[rows], sem.at[i]))
+        fetches[-1].start()
     gather_shifts(inner, planes, table, shift, blocks, INNER)
     gather_shifts(other, more, table, shift, blocks, INNER)
-    fetch.wait()
+    for fetch in fetches:
+        fetch.wait()
     convolve(before, inner, None, held, False)
 
 
@@ -263,9 +277,7 @@
     outer_other,
     *rest,
 ):
-    *outs, planes, grad, held, sem = rest
-    fetch = pltpu.make_async_copy(weight, held, sem)
-    fetch.start()
+    *outs, planes, grad = rest
     blocks, channels = hidden.shape[1], hidden.shape[3]
     step = blocks * ROWS
     for part, (field, target) in enumerate(((source, outer), (source_other, outer_other))):
@@ -275,13 +287,12 @@
             planes, blocks, got_first, got_second, pl.ds(part * channels, channels), (0, 1)
         )
         gather_shifts(target, planes, table, shift, blocks, OUTER)
-    fetch.wait()
     for x in range(4):
         value = before[x * step : (x + 1) * step, :]
         if x in (0, 3):
             for n in range(9):
                 taps = outer[n, :step, :] if x == 0 else outer[n, step:, :]
-                value += times(taps, tap_weight(held, n if x == 0 else 18 + n, False), False)
+                value += times(taps, tap_weight(weight, n if x == 0 else 18 + n, False), False)
         hidden[x] = jnp.maximum(value, 0.0).astype(BF16).reshape(hidden.shape[1:])
     left = hidden[...].reshape(4 * step, channels)
     emit_gradient(
@@ -342,14 +353,12 @@
             out[0, b, at, :] = value.astype(BF16)
 
 
-def unpack_kernel(factor, *refs):
-    ins, outs = refs[:-2], refs[-2:]
+def unpack_kernel(factor, keep, got, out):
     core = lax.rem(lax.axis_index("dp"), 2)
-    for keep, got, out in zip(ins[0::2], ins[1::2], outs):
-        columns = out.shape[0]
-        whole = (keep[...].astype(F32) + got[...].astype(F32)) * factor
-        whole = jnp.where(core == 0, whole, pltpu.roll(whole, columns, 1)).T
-        out[...] = jnp.concatenate([whole[:columns], whole[columns:]], axis=1)
+    columns = out.shape[0]
+    whole = (keep[...].astype(F32) + got[...].astype(F32)) * factor
+    whole = jnp.where(core == 0, whole, pltpu.roll(whole, columns, 1)).T
+    out[...] = jnp.concatenate([whole[:columns], whole[columns:]], axis=1)
 
 
 def call(kernel, outs, ins, places, scratch=(), limit=24, flops=0):
@@ -419,7 +428,7 @@
     two = swaps(keeps, sends, [LAST])
     keeps, sends = add_terms(one)
     one = swaps(keeps, sends, [LAST])
-    return [term[0] for term in one[0] + two[0]], results
+    return [[term[0] for term in part[0]] for part in (one, two)], results
 
 
 def per_device(
@@ -442,6 +451,7 @@
     else:
         shares = [array(taps_in, channels, dtype=F32)]
     edges = array(edge, ROWS, 2 * channels)
+    table = neighbour_table.transpose(1, 0, 2)
     planes = pltpu.VMEM((4, slots, ROWS, channels), BF16)
     ends = pltpu.VMEM((2, slots, ROWS, channels), BF16)
     inner_shape = array(9, 4 * blocks * ROWS, channels)
@@ -459,19 +469,19 @@
     around = array(4, slots, ROWS, channels)
     first, second, shift, source, source_other = call(
         pack_kernel,
-        [edges, edges, array(8 * ROWS, 9 * ROWS), around, around],
-        (send_lists, features, cotangent),
-        "shh",
+        [edges, edges, array(16 * ROWS, 12 * ROWS), around, around],
+        (send_lists, jnp.concatenate([features, cotangent])),
+        "sh",
         [sem((2, 4))],
         limit=6,
     )
     got_first, got_second = swap_halos(first, second)
-    inner, inner_other, before = call(
+    inner, inner_other, before, held_one = call(
         inner_kernel,
-        [inner_shape, inner_shape, total],
-        (neighbour_table, source, source_other, shift, weight_one),
+        [inner_shape, inner_shape, total, held],
+        (table, source, source_other, shift, weight_one),
         "svvvh",
-        [scratch(held), sem],
+        [sem((3,))],
         limit=INNER_LIMIT,
         flops=2 * product,
     )
@@ -479,19 +489,19 @@
         functools.partial(forward_kernel, packed, ORDERS_TWO),
         [field, outer_shape, outer_shape] + shares,
         (
-            neighbour_table,
+            table,
             source,
             source_other,
             got_first,
             got_second,
             shift,
-            weight_one,
+            held_one,
             inner,
             inner_other,
             before,
         ),
-        "svvvvvhvvv",
-        [ends, full, scratch(held), sem],
+        "svvvvvvvvv",
+        [ends, full],
         limit=FORWARD_LIMIT,
         flops=2 * product,
     )
@@ -525,7 +535,7 @@
             functools.partial(second_kernel, part, part == 1, len(tokens)),
             [array(*features.shape)],
             (
-                neighbour_table,
+                table,
                 block_counts,
                 source,
                 got_first,
@@ -555,10 +565,8 @@
         )
         out = array(channels // dp_size, taps_in // slab_size, dtype=F32)
         grad_one, grad_two = (
-            turned.T
-            for turned in call(
-                functools.partial(unpack_kernel, factor), [out, out], terms, "v" * len(terms)
-            )
+            call(functools.partial(unpack_kernel, factor), [out], pair, "vv")[0].T
+            for pair in terms
         )
     else:
         halos = swap_halos(first, second)

time: 80.7 us -> 78 us (0.967)
  local copies, waits for them, and re-layouts: 3.94 us -> 1.3 us
  waiting for transfers between devices: 12.9 us -> 11.7 us
  other arithmetic: 1.26 us -> 2.43 us
    unnamed x17 -> x14, local copies, waits for them, and re-layouts: 3.34 us -> 0.71 us
    ppermute x14, waiting for transfers between devices: 12.9 us -> 11.7 us  [swap(): lax.ppermute(array, ('dp', 'slab'), pair_perm(name, dp_size, slab_size))]
    concatenate x0 -> x1, other arithmetic: none -> 1.14 us  [per_device(): jnp.concatenate([features, cotangent])]
    pallas_call x8 -> x9, Pallas kernels: 31.8 us -> 31.8 us  [call(): pl.pallas_call(kernel, out_shape=outs, in_specs=[pl.BlockSpec(memory_spac...]
  transfers between devices with their start and end apart: 18 -> 18, of which waited for: 5 -> 5; matrix products, arithmetic and copies ran while one was open for 3% -> 2% of each run, Pallas kernels for 29% -> 31%
where the time goes in v1:
time: 78 us; the launch traced here: 77.8 us
  Pallas kernels  31.8 us (41%)
  starting transfers between devices  28.9 us (37%)
  waiting for transfers between devices  11.7 us (15%)
  other arithmetic  2.43 us (3%)
  between operations  1.67 us (2%)
  local copies, waits for them, and re-layouts  1.3 us (2%)
    pallas_call x9, Pallas kernels, call(): pl.pallas_call(kernel, out_shape=outs, in_specs=[pl.BlockSpec(memory_spac...  31.8 us
    ppermute x14, starting transfers between devices, swap(): lax.ppermute(array, ('dp', 'slab'), pair_perm(name, dp_size, slab_size))  20.1 us
    ppermute x14, waiting for transfers between devices, swap(): lax.ppermute(array, ('dp', 'slab'), pair_perm(name, dp_size, slab_size))  11.7 us
    ppermute x2, starting transfers between devices, swap_halos(): lax.ppermute(first, 'slab', even)  7.35 us
  transfers between devices with their start and end apart: 18, of which 5 were waited for; matrix products, arithmetic and copies ran while one was open for 2% of the time, Pallas kernels for 31%

profile of v1, /device:TPU:0, one launch (start us, length us, event | category | flops | bytes accessed | tf_op | source)
XLA Modules:
  0.0 77.8 jit_solution(11090198742753635768)
XLA Ops:
  0.6 1.1 %pad_maximum_fusion.fields = bf16[2,10,64,256]{3,2,1,0:T(8,128)(2,1)S(1)} fusion(bf16[1,10,64,256]{3,2,1,0:T(8,128)(2,1)} %rows.3, bf16[1,10,64,256]{3,2,1,0:T(8,128)(2,1)} %rows.2), kind=kLoop, calls=%fused_computation.3 | loop fusion | flops 327680 | bytes 1310720 | tf_op jit(solution)/shard_map/concatenate | solution.py:473
  1.8 0.7 copy-done.2
  2.5 0.9 %shard_map.102 = (bf16[2,16,512]{2,1,0:T(8,128)(2,1)S(1)}, bf16[2,16,512]{2,1,0:T(8,128)(2,1)S(1)}, bf16[256,192]{1,0:T(8,128)(2,1)S(1)}, bf16[4,15,16,256]{3,2,...) custom-call(s32[1,1,2,2]{3,2,1,0:T(2,128)S(1)} %copy-done.2, bf16[2,10,64,256]{3,2,1,0:T(8,128)(2,1)S(1)} %pad_maximum_fusion.fields), custom_call_target="tpu_custom_call" | custom-call | tf_op jit(solution)/shard_map/pallas_call | solution.py:366
  3.4 3.0 %collective-permute-start = (bf16[2,16,512]{2,1,0:T(8,128)(2,1)S(1)}, bf16[2,16,512]{2,1,0:T(8,128)(2,1)S(1)}, u32[]{:S(2)}, u32[]{:S(2)}) collective-permute-start(bf16[2,16,512]{2,1,0:T(8,128)(2,1)S(1)} %get-tuple-element.46), channel_id=1, source_target_pairs={{0,1},{1,0},{2,3},{3,2},{4,5},{5,4},{6,7},{7,6},{8,9},{9,8},{10,11... | collective-permute-start | bytes 98312 | tf_op jit(solution)/shard_map/ppermute | solution.py:75
  6.4 0.7 collective-permute-start.1
  7.1 4.8 %shard_map.103 = (bf16[9,640,256]{2,1,0:T(8,128)(2,1)S(1)}, bf16[9,640,256]{2,1,0:T(8,128)(2,1)S(1)}, f32[640,256]{1,0:T(8,128)S(1)}, bf16[6912,256]{1,0:T(8,128)(2,1)S(1)}) custom-call(s32[10,1,27]{2,1,0:T(1,128)S(1)} %bitcast.11, bf16[4,15,16,256]{3,2,1,0:T(8,128)(2,1)S(1)} %get-tuple-element.44.planes.source, ...), custom_call_target="tpu_custom_call" | custom-call | flops 4529848320 | tf_op jit(solution)/shard_map/pallas_call | solution.py:366
  12.0 6.0 %shard_map.104 = (bf16[4,10,16,256]{3,2,1,0:T(8,128)(2,1)S(1)}, bf16[9,320,256]{2,1,0:T(8,128)(2,1)S(1)}, bf16[9,320,256]{2,1,0:T(8,128)(2,1)S(1)}, bf16[16,432,...) custom-call(s32[10,1,27]{2,1,0:T(1,128)S(1)} %bitcast.12, bf16[4,15,16,256]{3,2,1,0:T(8,128)(2,1)S(1)} %get-tuple-element.44.planes.source, ...), custom_call_target="tpu_custom_call" | custom-call | flops 4529848320 | tf_op jit(solution)/shard_map/pallas_call | solution.py:366
  18.1 3.0 %shard_map.105 = (bf16[4,10,16,256]{3,2,1,0:T(8,128)(2,1)S(1)}, bf16[2,16,512]{2,1,0:T(8,128)(2,1)S(1)}, bf16[2,16,512]{2,1,0:T(8,128)(2,1)S(1)}) custom-call(s32[1,1,2,2]{3,2,1,0:T(2,128)S(1)} %copy-done.3, bf16[9,640,256]{2,1,0:T(8,128)(2,1)S(1)} %get-tuple-element.51.other.inner, bf16[9,320,256]{2,1,0:T(8,128)(2,1)S(1)} %get-tuple-element.56.outer, ...), custom_call_target="tpu_custom_call" | custom-call | flops 2264924160 | tf_op jit(solution)/shard_map/pallas_call | solution.py:366
  21.1 3.4 %shard_map.106 = (bf16[16,432,128]{2,1,0:T(8,128)(2,1)S(1)}, bf16[16,432,128]{2,1,0:T(8,128)(2,1)S(1)}) custom-call(bf16[9,640,256]{2,1,0:T(8,128)(2,1)S(1)} %get-tuple-element.50.inner, bf16[9,320,256]{2,1,0:T(8,128)(2,1)S(1)} %get-tuple-element.59.outer, bf16[4,10,16,256]{3,2,1,0:T(8,128)(2,1)S(1)} %get-tuple-element.60.grad_hidden.source), custom_call_target="tpu_custom_call" | custom-call | flops 2264924160 | tf_op jit(solution)/shard_map/pallas_call | solution.py:366
  24.5 0.5 collective-permute-start.5
  25.9 4.4 %collective-permute-start.3 = (bf16[2,16,512]{2,1,0:T(8,128)(2,1)S(1)}, bf16[2,16,512]{2,1,0:T(8,128)(2,1)S(1)}, u32[]{:S(2)}, u32[]{:S(2)}) collective-permute-start(bf16[2,16,512]{2,1,0:T(8,128)(2,1)S(1)} %get-tuple-element.57), channel_id=1, source_target_pairs={{0,1},{1,0},{2,3},{3,2},{4,5},{5,4},{6,7},{7,6},{8,9},{9,8},{10,11... | collective-permute-start | bytes 98312 | tf_op jit(solution)/shard_map/ppermute | solution.py:75
  30.2 0.8 %collective-permute-start.4 = (bf16[2,16,512]{2,1,0:T(8,128)(2,1)S(1)}, bf16[2,16,512]{2,1,0:T(8,128)(2,1)S(1)}, u32[]{:S(2)}, u32[]{:S(2)}) collective-permute-start(bf16[2,16,512]{2,1,0:T(8,128)(2,1)S(1)} %get-tuple-element.58), channel_id=1, source_target_pairs={{1,2},{2,1},{3,4},{4,3},{5,6},{6,5},{9,10},{10,9},{11,12},{12,11},... | collective-permute-start | bytes 98312 | tf_op jit(solution)/shard_map/ppermute | solution.py:75
  31.7 1.6 %collective-permute-start.7 = (bf16[8,176,128]{2,1,0:T(8,128)(2,1)S(1)}, bf16[8,176,128]{2,1,0:T(8,128)(2,1)S(1)}, u32[]{:S(2)}, u32[]{:S(2)}) collective-permute-start(bf16[8,176,128]{2,1,0:T(8,128)(2,1)S(1)} %get-tuple-element.69), channel_id=1, source_target_pairs={{0,16},{1,17},{2,18},{3,19},{4,20},{5,21},{6,22},{7,23},{8,24},{9,... | collective-permute-start | bytes 1081352 | tf_op jit(solution)/shard_map/ppermute | solution.py:68
  33.3 4.3 %collective-permute-start.6 = (bf16[8,256,128]{2,1,0:T(8,128)(2,1)S(1)}, bf16[8,256,128]{2,1,0:T(8,128)(2,1)S(1)}, u32[]{:S(2)}, u32[]{:S(2)}) collective-permute-start(bf16[8,256,128]{2,1,0:T(8,128)(2,1)S(1)} %get-tuple-element.67), channel_id=1, source_target_pairs={{0,1},{1,0},{2,3},{3,2},{4,5},{5,4},{6,7},{7,6},{8,9},{9,8},{10,11... | collective-permute-start | bytes 1572872 | tf_op jit(solution)/shard_map/ppermute | solution.py:68
  37.7 0.6 collective-permute-start.9
  38.3 1.6 %collective-permute-start.8 = (bf16[8,288,128]{2,1,0:T(8,128)(2,1)S(1)}, bf16[8,288,128]{2,1,0:T(8,128)(2,1)S(1)}, u32[]{:S(2)}, u32[]{:S(2)}) collective-permute-start(bf16[8,288,128]{2,1,0:T(8,128)(2,1)S(1)} %get-tuple-element.85.rest_0_), channel_id=1, source_target_pairs={{0,2},{1,3},{2,0},{3,1},{4,6},{5,7},{6,4},{7,5},{8,10},{9,11},{10,... | collective-permute-start | bytes 1769480 | tf_op jit(solution)/shard_map/ppermute | solution.py:68
  39.9 5.8 %shard_map.107 = bf16[1,10,64,256]{3,2,1,0:T(8,128)(2,1)} custom-call(s32[10,1,27]{2,1,0:T(1,128)S(1)} %bitcast.13, s32[1,1]{1,0:T(1,128)S(6)} %copy.11.counts, bf16[4,10,16,256]{3,2,1,0:T(8,128)(2,1)S(1)} %get-tuple-element.55.hidden.source, bf16[2,16,512]{2,1,0:T(8,128)(2,1)S(1)} %collective-permute-done.3.got_first, ...), custom_call_target="tpu_custom_call" | custom-call | flops 2264924160 | tf_op jit(solution)/shard_map/pallas_call | solution.py:366
  45.8 3.0 %collective-permute-done.6 = bf16[8,256,128]{2,1,0:T(8,128)(2,1)S(1)} collective-permute-done((bf16[8,256,128]{2,1,0:T(8,128)(2,1)S(1)}, bf16[8,256,128]{2,1,0:T(8,128)(2,1)S(1)}, u32[]{:S(2)}, u32[]{:S(2)}) %collective-permute-start.6) | collective-permute-done | bytes 524320 | tf_op jit(solution)/shard_map/ppermute | solution.py:68
  49.0 0.6 collective-permute-start.10
  49.6 1.7 %collective-permute-start.11 = (bf16[4,176,128]{2,1,0:T(8,128)(2,1)S(1)}, bf16[4,176,128]{2,1,0:T(8,128)(2,1)S(1)}, u32[]{:S(2)}, u32[]{:S(2)}) collective-permute-start(bf16[4,176,128]{2,1,0:T(8,128)(2,1)S(1)} %get-tuple-element.76), channel_id=1, source_target_pairs={{0,1},{1,0},{2,3},{3,2},{4,5},{5,4},{6,7},{7,6},{8,9},{9,8},{10,11... | collective-permute-start | bytes 540680 | tf_op jit(solution)/shard_map/ppermute | solution.py:68
  51.5 1.6 %collective-permute-start.13 = (bf16[4,144,128]{2,1,0:T(8,128)(2,1)S(1)}, bf16[4,144,128]{2,1,0:T(8,128)(2,1)S(1)}, u32[]{:S(2)}, u32[]{:S(2)}) collective-permute-start(bf16[4,144,128]{2,1,0:T(8,128)(2,1)S(1)} %get-tuple-element.103.rest_1_), channel_id=1, source_target_pairs={{0,2},{1,3},{2,0},{3,1},{4,6},{5,7},{6,4},{7,5},{8,10},{9,11},{10,... | collective-permute-start | bytes 442376 | tf_op jit(solution)/shard_map/ppermute | solution.py:68
  53.3 1.6 %collective-permute-start.12 = (bf16[4,288,128]{2,1,0:T(8,128)(2,1)S(1)}, bf16[4,288,128]{2,1,0:T(8,128)(2,1)S(1)}, u32[]{:S(2)}, u32[]{:S(2)}) collective-permute-start(bf16[4,288,128]{2,1,0:T(8,128)(2,1)S(1)} %get-tuple-element.91.rest_0_), channel_id=1, source_target_pairs={{0,16},{1,17},{2,18},{3,19},{4,20},{5,21},{6,22},{7,23},{8,24},{9,... | collective-permute-start | bytes 884744 | tf_op jit(solution)/shard_map/ppermute | solution.py:68
  54.9 5.8 %shard_map.108 = bf16[1,10,64,256]{3,2,1,0:T(8,128)(2,1)} custom-call(s32[10,1,27]{2,1,0:T(1,128)S(1)} %bitcast.14, s32[1,1]{1,0:T(1,128)S(6)} %copy.11.counts, bf16[4,10,16,256]{3,2,1,0:T(8,128)(2,1)S(1)} %get-tuple-element.60.grad_hidden.source, bf16[2,16,512]{2,1,0:T(8,128)(2,1)S(1)} %collective-permute-done.3.got_first, ...), custom_call_target="tpu_custom_call" | custom-call | flops 2264924160 | tf_op jit(solution)/shard_map/pallas_call | solution.py:366
  60.9 0.9 %collective-permute-start.14 = (bf16[2,432,128]{2,1,0:T(8,128)(2,1)S(1)}, bf16[2,432,128]{2,1,0:T(8,128)(2,1)S(1)}, u32[]{:S(2)}, u32[]{:S(2)}) collective-permute-start(bf16[2,432,128]{2,1,0:T(8,128)(2,1)S(1)} %get-tuple-element.80), channel_id=1, source_target_pairs={{0,2},{1,3},{2,0},{3,1},{4,6},{5,7},{6,4},{7,5},{8,10},{9,11},{10,... | collective-permute-start | bytes 663560 | tf_op jit(solution)/shard_map/ppermute | solution.py:68
  61.8 0.4 collective-permute-done.12
  62.4 2.0 %collective-permute-start.15 = (bf16[2,432,128]{2,1,0:T(8,128)(2,1)S(1)}, bf16[2,432,128]{2,1,0:T(8,128)(2,1)S(1)}, u32[]{:S(2)}, u32[]{:S(2)}) collective-permute-start(bf16[2,432,128]{2,1,0:T(8,128)(2,1)S(1)} %get-tuple-element.82), channel_id=1, source_target_pairs={{0,1},{1,0},{2,3},{3,2},{4,5},{5,4},{6,7},{7,6},{8,9},{9,8},{10,11... | collective-permute-start | bytes 663560 | tf_op jit(solution)/shard_map/ppermute | solution.py:68
  64.4 3.4 %collective-permute-done.14 = bf16[2,432,128]{2,1,0:T(8,128)(2,1)S(1)} collective-permute-done((bf16[2,432,128]{2,1,0:T(8,128)(2,1)S(1)}, bf16[2,432,128]{2,1,0:T(8,128)(2,1)S(1)}, u32[]{:S(2)}, u32[]{:S(2)}) %collective-permute-start.14) | collective-permute-done | bytes 221216 | tf_op jit(solution)/shard_map/ppermute | solution.py:68
  67.8 2.0 %collective-permute-start.17 = (bf16[1,432,128]{2,1,0:T(8,128)(2,1)S(1)}, bf16[1,432,128]{2,1,0:T(8,128)(2,1)S(1)}, u32[]{:S(2)}, u32[]{:S(2)}) collective-permute-start(bf16[1,432,128]{2,1,0:T(8,128)(2,1)S(1)} %get-tuple-element.83), channel_id=1, source_target_pairs={{0,4},{1,5},{2,6},{3,7},{4,0},{5,1},{6,2},{7,3},{8,12},{9,13},{10,... | collective-permute-start | bytes 331784 | tf_op jit(solution)/shard_map/ppermute | solution.py:68
  69.9 1.1 %collective-permute-start.16 = (bf16[1,432,128]{2,1,0:T(8,128)(2,1)S(1)}, bf16[1,432,128]{2,1,0:T(8,128)(2,1)S(1)}, u32[]{:S(2)}, u32[]{:S(2)}) collective-permute-start(bf16[1,432,128]{2,1,0:T(8,128)(2,1)S(1)} %get-tuple-element.106), channel_id=1, source_target_pairs={{0,4},{1,5},{2,6},{3,7},{4,0},{5,1},{6,2},{7,3},{8,12},{9,13},{10,... | collective-permute-start | bytes 331784 | tf_op jit(solution)/shard_map/ppermute | solution.py:68
  70.9 4.7 %collective-permute-done.17 = bf16[1,432,128]{2,1,0:T(8,128)(2,1)S(1)} collective-permute-done((bf16[1,432,128]{2,1,0:T(8,128)(2,1)S(1)}, bf16[1,432,128]{2,1,0:T(8,128)(2,1)S(1)}, u32[]{:S(2)}, u32[]{:S(2)}) %collective-permute-start.17) | collective-permute-done | bytes 110624 | tf_op jit(solution)/shard_map/ppermute | solution.py:68
  75.7 1.0 %shard_map.110 = f32[64,864]{1,0:T(8,128)} custom-call(bf16[432,128]{1,0:T(8,128)(2,1)S(1)} %get-tuple-element.104.keep, bf16[432,128]{1,0:T(8,128)(2,1)S(1)} %bitcast.9), custom_call_target="tpu_custom_call" | custom-call | tf_op jit(solution)/shard_map/pallas_call | solution.py:366
  76.9 1.0 %shard_map.109 = f32[64,864]{1,0:T(8,128)} custom-call(bf16[432,128]{1,0:T(8,128)(2,1)S(1)} %get-tuple-element.107.keep, bf16[432,128]{1,0:T(8,128)(2,1)S(1)} %bitcast.10), custom_call_target="tpu_custom_call" | custom-call | tf_op jit(solution)/shard_map/pallas_call | solution.py:366
  (54 shorter events, 2.2 us)
Async XLA Ops:
  0.6 6.4 %copy-start.6 = (s32[1,10,27]{2,0,1:T(1,128)S(1)}, s32[1,10,27]{2,0,1:T(1,128)}, u32[]{:S(2)}) copy-start(s32[1,10,27]{2,0,1:T(1,128)} %param.9) | copy-start | bytes 3244
  1.8 0.7 copy-start.2
  3.4 8.5 %collective-permute-start = (bf16[2,16,512]{2,1,0:T(8,128)(2,1)S(1)}, bf16[2,16,512]{2,1,0:T(8,128)(2,1)S(1)}, u32[]{:S(2)}, u32[]{:S(2)}) collective-permute-start(bf16[2,16,512]{2,1,0:T(8,128)(2,1)S(1)} %get-tuple-element.46), channel_id=1, source_target_pairs={{0,1},{1,0},{2,3},{3,2},{4,5},{5,4},{6,7},{7,6},{8,9},{9,8},{10,11... | collective-permute-start | bytes 98312 | tf_op jit(solution)/shard_map/ppermute | solution.py:75
  6.4 5.5 %collective-permute-start.1 = (bf16[2,16,512]{2,1,0:T(8,128)(2,1)S(1)}, bf16[2,16,512]{2,1,0:T(8,128)(2,1)S(1)}, u32[]{:S(2)}, u32[]{:S(2)}) collective-permute-start(bf16[2,16,512]{2,1,0:T(8,128)(2,1)S(1)} %get-tuple-element.47), channel_id=1, source_target_pairs={{1,2},{2,1},{3,4},{4,3},{5,6},{6,5},{9,10},{10,9},{11,12},{12,11},... | collective-permute-start | bytes 98312 | tf_op jit(solution)/shard_map/ppermute | solution.py:75
  12.0 6.1 %copy-start.3 = (s32[1,1,2,2]{3,2,1,0:T(2,128)S(1)}, s32[1,1,2,2]{3,2,1,0:T(2,128)}, u32[]{:S(2)}) copy-start(s32[1,1,2,2]{3,2,1,0:T(2,128)} %lists.3) | copy-start | bytes 52
  12.0 6.1 %copy-start.4 = (bf16[6912,256]{1,0:T(8,128)(2,1)S(1)}, bf16[6912,256]{1,0:T(8,128)(2,1)}, u32[]{:S(2)}) copy-start(bf16[6912,256]{1,0:T(8,128)(2,1)} %weight.6) | copy-start | bytes 10616836
  18.0 13.1 %collective-permute-start.2 = (bf16[16,432,128]{2,1,0:T(8,128)(2,1)S(1)}, bf16[16,432,128]{2,1,0:T(8,128)(2,1)S(1)}, u32[]{:S(2)}, u32[]{:S(2)}) collective-permute-start(bf16[16,432,128]{2,1,0:T(8,128)(2,1)S(1)} %get-tuple-element.54), channel_id=1, source_target_pairs={{0,8},{1,9},{2,10},{3,11},{4,12},{5,13},{6,14},{7,15},{8,0},{9,1},... | collective-permute-start | bytes 5308424 | tf_op jit(solution)/shard_map/ppermute | solution.py:68
  24.5 6.9 %collective-permute-start.5 = (bf16[16,432,128]{2,1,0:T(8,128)(2,1)S(1)}, bf16[16,432,128]{2,1,0:T(8,128)(2,1)S(1)}, u32[]{:S(2)}, u32[]{:S(2)}) collective-permute-start(bf16[16,432,128]{2,1,0:T(8,128)(2,1)S(1)} %get-tuple-element.63), channel_id=1, source_target_pairs={{0,8},{1,9},{2,10},{3,11},{4,12},{5,13},{6,14},{7,15},{8,0},{9,1},... | collective-permute-start | bytes 5308424 | tf_op jit(solution)/shard_map/ppermute | solution.py:68
  25.9 12.4 %collective-permute-start.3 = (bf16[2,16,512]{2,1,0:T(8,128)(2,1)S(1)}, bf16[2,16,512]{2,1,0:T(8,128)(2,1)S(1)}, u32[]{:S(2)}, u32[]{:S(2)}) collective-permute-start(bf16[2,16,512]{2,1,0:T(8,128)(2,1)S(1)} %get-tuple-element.57), channel_id=1, source_target_pairs={{0,1},{1,0},{2,3},{3,2},{4,5},{5,4},{6,7},{7,6},{8,9},{9,8},{10,11... | collective-permute-start | bytes 98312 | tf_op jit(solution)/shard_map/ppermute | solution.py:75
  30.2 9.6 %collective-permute-start.4 = (bf16[2,16,512]{2,1,0:T(8,128)(2,1)S(1)}, bf16[2,16,512]{2,1,0:T(8,128)(2,1)S(1)}, u32[]{:S(2)}, u32[]{:S(2)}) collective-permute-start(bf16[2,16,512]{2,1,0:T(8,128)(2,1)S(1)} %get-tuple-element.58), channel_id=1, source_target_pairs={{1,2},{2,1},{3,4},{4,3},{5,6},{6,5},{9,10},{10,9},{11,12},{12,11},... | collective-permute-start | bytes 98312 | tf_op jit(solution)/shard_map/ppermute | solution.py:75
  31.7 8.2 %copy-start = (bf16[1,10,64,256]{3,2,1,0:T(8,128)(2,1)S(1)}, bf16[1,10,64,256]{3,2,1,0:T(8,128)(2,1)}, u32[]{:S(2)}) copy-start(bf16[1,10,64,256]{3,2,1,0:T(8,128)(2,1)} %rows.2) | copy-start | bytes 983044
  31.7 14.0 %collective-permute-start.7 = (bf16[8,176,128]{2,1,0:T(8,128)(2,1)S(1)}, bf16[8,176,128]{2,1,0:T(8,128)(2,1)S(1)}, u32[]{:S(2)}, u32[]{:S(2)}) collective-permute-start(bf16[8,176,128]{2,1,0:T(8,128)(2,1)S(1)} %get-tuple-element.69), channel_id=1, source_target_pairs={{0,16},{1,17},{2,18},{3,19},{4,20},{5,21},{6,22},{7,23},{8,24},{9,... | collective-permute-start | bytes 1081352 | tf_op jit(solution)/shard_map/ppermute | solution.py:68
  33.3 15.6 %collective-permute-start.6 = (bf16[8,256,128]{2,1,0:T(8,128)(2,1)S(1)}, bf16[8,256,128]{2,1,0:T(8,128)(2,1)S(1)}, u32[]{:S(2)}, u32[]{:S(2)}) collective-permute-start(bf16[8,256,128]{2,1,0:T(8,128)(2,1)S(1)} %get-tuple-element.67), channel_id=1, source_target_pairs={{0,1},{1,0},{2,3},{3,2},{4,5},{5,4},{6,7},{7,6},{8,9},{9,8},{10,11... | collective-permute-start | bytes 1572872 | tf_op jit(solution)/shard_map/ppermute | solution.py:68
  37.7 13.7 %collective-permute-start.9 = (bf16[8,144,128]{2,1,0:T(8,128)(2,1)S(1)}, bf16[8,144,128]{2,1,0:T(8,128)(2,1)S(1)}, u32[]{:S(2)}, u32[]{:S(2)}) collective-permute-start(bf16[8,144,128]{2,1,0:T(8,128)(2,1)S(1)} %get-tuple-element.93.rest_1_), channel_id=1, source_target_pairs={{0,16},{1,17},{2,18},{3,19},{4,20},{5,21},{6,22},{7,23},{8,24},{9,... | collective-permute-start | bytes 884744 | tf_op jit(solution)/shard_map/ppermute | solution.py:68
  38.3 14.8 %collective-permute-start.8 = (bf16[8,288,128]{2,1,0:T(8,128)(2,1)S(1)}, bf16[8,288,128]{2,1,0:T(8,128)(2,1)S(1)}, u32[]{:S(2)}, u32[]{:S(2)}) collective-permute-start(bf16[8,288,128]{2,1,0:T(8,128)(2,1)S(1)} %get-tuple-element.85.rest_0_), channel_id=1, source_target_pairs={{0,2},{1,3},{2,0},{3,1},{4,6},{5,7},{6,4},{7,5},{8,10},{9,11},{10,... | collective-permute-start | bytes 1769480 | tf_op jit(solution)/shard_map/ppermute | solution.py:68
  49.0 11.7 %collective-permute-start.10 = (bf16[4,256,128]{2,1,0:T(8,128)(2,1)S(1)}, bf16[4,256,128]{2,1,0:T(8,128)(2,1)S(1)}, u32[]{:S(2)}, u32[]{:S(2)}) collective-permute-start(bf16[4,256,128]{2,1,0:T(8,128)(2,1)S(1)} %get-tuple-element.75), channel_id=1, source_target_pairs={{0,16},{1,17},{2,18},{3,19},{4,20},{5,21},{6,22},{7,23},{8,24},{9,... | collective-permute-start | bytes 786440 | tf_op jit(solution)/shard_map/ppermute | solution.py:68
  49.6 11.1 %collective-permute-start.11 = (bf16[4,176,128]{2,1,0:T(8,128)(2,1)S(1)}, bf16[4,176,128]{2,1,0:T(8,128)(2,1)S(1)}, u32[]{:S(2)}, u32[]{:S(2)}) collective-permute-start(bf16[4,176,128]{2,1,0:T(8,128)(2,1)S(1)} %get-tuple-element.76), channel_id=1, source_target_pairs={{0,1},{1,0},{2,3},{3,2},{4,5},{5,4},{6,7},{7,6},{8,9},{9,8},{10,11... | collective-permute-start | bytes 540680 | tf_op jit(solution)/shard_map/ppermute | solution.py:68
  51.4 3.6 %copy-start.5 = (bf16[6912,256]{1,0:T(8,128)(2,1)S(1)}, bf16[6912,256]{1,0:T(8,128)(2,1)}, u32[]{:S(2)}) copy-start(bf16[6912,256]{1,0:T(8,128)(2,1)} %weight.7) | copy-start | bytes 10616836
  51.5 3.5 %copy-start.1 = (bf16[1,10,64,256]{3,2,1,0:T(8,128)(2,1)S(1)}, bf16[1,10,64,256]{3,2,1,0:T(8,128)(2,1)}, u32[]{:S(2)}) copy-start(bf16[1,10,64,256]{3,2,1,0:T(8,128)(2,1)} %rows.3) | copy-start | bytes 983044
  51.5 10.3 %collective-permute-start.13 = (bf16[4,144,128]{2,1,0:T(8,128)(2,1)S(1)}, bf16[4,144,128]{2,1,0:T(8,128)(2,1)S(1)}, u32[]{:S(2)}, u32[]{:S(2)}) collective-permute-start(bf16[4,144,128]{2,1,0:T(8,128)(2,1)S(1)} %get-tuple-element.103.rest_1_), channel_id=1, source_target_pairs={{0,2},{1,3},{2,0},{3,1},{4,6},{5,7},{6,4},{7,5},{8,10},{9,11},{10,... | collective-permute-start | bytes 442376 | tf_op jit(solution)/shard_map/ppermute | solution.py:68
  53.3 8.9 %collective-permute-start.12 = (bf16[4,288,128]{2,1,0:T(8,128)(2,1)S(1)}, bf16[4,288,128]{2,1,0:T(8,128)(2,1)S(1)}, u32[]{:S(2)}, u32[]{:S(2)}) collective-permute-start(bf16[4,288,128]{2,1,0:T(8,128)(2,1)S(1)} %get-tuple-element.91.rest_0_), channel_id=1, source_target_pairs={{0,16},{1,17},{2,18},{3,19},{4,20},{5,21},{6,22},{7,23},{8,24},{9,... | collective-permute-start | bytes 884744 | tf_op jit(solution)/shard_map/ppermute | solution.py:68
  60.9 6.8 %collective-permute-start.14 = (bf16[2,432,128]{2,1,0:T(8,128)(2,1)S(1)}, bf16[2,432,128]{2,1,0:T(8,128)(2,1)S(1)}, u32[]{:S(2)}, u32[]{:S(2)}) collective-permute-start(bf16[2,432,128]{2,1,0:T(8,128)(2,1)S(1)} %get-tuple-element.80), channel_id=1, source_target_pairs={{0,2},{1,3},{2,0},{3,1},{4,6},{5,7},{6,4},{7,5},{8,10},{9,11},{10,... | collective-permute-start | bytes 663560 | tf_op jit(solution)/shard_map/ppermute | solution.py:68
  62.4 7.4 %collective-permute-start.15 = (bf16[2,432,128]{2,1,0:T(8,128)(2,1)S(1)}, bf16[2,432,128]{2,1,0:T(8,128)(2,1)S(1)}, u32[]{:S(2)}, u32[]{:S(2)}) collective-permute-start(bf16[2,432,128]{2,1,0:T(8,128)(2,1)S(1)} %get-tuple-element.82), channel_id=1, source_target_pairs={{0,1},{1,0},{2,3},{3,2},{4,5},{5,4},{6,7},{7,6},{8,9},{9,8},{10,11... | collective-permute-start | bytes 663560 | tf_op jit(solution)/shard_map/ppermute | solution.py:68
  67.8 7.9 %collective-permute-start.17 = (bf16[1,432,128]{2,1,0:T(8,128)(2,1)S(1)}, bf16[1,432,128]{2,1,0:T(8,128)(2,1)S(1)}, u32[]{:S(2)}, u32[]{:S(2)}) collective-permute-start(bf16[1,432,128]{2,1,0:T(8,128)(2,1)S(1)} %get-tuple-element.83), channel_id=1, source_target_pairs={{0,4},{1,5},{2,6},{3,7},{4,0},{5,1},{6,2},{7,3},{8,12},{9,13},{10,... | collective-permute-start | bytes 331784 | tf_op jit(solution)/shard_map/ppermute | solution.py:68
  69.9 7.0 %collective-permute-start.16 = (bf16[1,432,128]{2,1,0:T(8,128)(2,1)S(1)}, bf16[1,432,128]{2,1,0:T(8,128)(2,1)S(1)}, u32[]{:S(2)}, u32[]{:S(2)}) collective-permute-start(bf16[1,432,128]{2,1,0:T(8,128)(2,1)S(1)} %get-tuple-element.106), channel_id=1, source_target_pairs={{0,4},{1,5},{2,6},{3,7},{4,0},{5,1},{6,2},{7,3},{8,12},{9,13},{10,... | collective-permute-start | bytes 331784 | tf_op jit(solution)/shard_map/ppermute | solution.py:68

commit v2 on v1

--- a/solution.py
+++ b/solution.py
@@ -18,14 +18,8 @@
 FORWARD_LIMIT = 14
 UNROLL = 5
 
-ORDERS_ONE = (
-    (0, 288, ("z1", "y", "x")),
-    (288, 432, ("y", "z1", "x")),
-)
-ORDERS_TWO = (
-    (0, 256, ("x", "y", "z1")),
-    (256, 432, ("y", "x", "z1")),
-)
+ORDERS_ONE = (("z1", "y", "x"), ("y", "z1", "x")), (2, 3)
+ORDERS_TWO = (("x", "y", "z1"), ("y", "x", "z1")), (3, 5)
 LAST = "z2"
 
 
@@ -43,6 +37,12 @@
     return jnp.where(column == source + 96 * (row >> 7), 1.0, 0.0).astype(BF16)
 
 
+def portions_of(rows, plan):
+    (order, other), (part, whole) = plan
+    at = rows * part // whole // ROWS * ROWS
+    return ((0, at, order), (at, rows, other))
+
+
 def bit_of(name, dp_index, slab_index):
     if name == "y":
         return dp_index // 2
@@ -75,9 +75,11 @@
     return lax.ppermute(first, "slab", even), lax.ppermute(second, "slab", odd)
 
 
-def pack_kernel(lists, fields, first, second, shift, planes, more, sems):
+def pack_kernel(far_lists, fields, first, second, shift, planes, more, sems, lists, sem):
     blocks = fields.shape[1]
-    copies = start_planes(planes, fields.at[0:1], blocks, sems.at[0])
+    copies = [pltpu.make_async_copy(far_lists, lists, sem)]
+    copies[0].start()
+    copies += start_planes(planes, fields.at[0:1], blocks, sems.at[0])
     copies += start_planes(more, fields.at[1:2], blocks, sems.at[1])
     shift[...] = shift_matrix()
     for field in (planes, more):
@@ -374,14 +376,18 @@
     )(*ins)
 
 
-def halves(array):
-    half = array.shape[0] // 2
-    return array[:half], array[half:]
-
-
 def add_terms(parts):
-    pairs = [halves(keep + got) for keep, got in parts]
-    return [keep for keep, _ in pairs], [send for _, send in pairs]
+    keeps, sends = [], []
+    for keep, got in parts:
+        half = keep.shape[0] // 2
+        sends.append(keep[half:] + got[half:])
+        keeps.append(keep[:half] + got[:half])
+    return keeps, sends
+
+
+def cut(parts, orders):
+    ((keep, got),) = parts
+    return [[keep[:, first:last], got[:, first:last]] for first, last, _ in orders]
 
 
 def swaps(keeps, sends, names):
@@ -397,23 +403,19 @@
     return [[keep, got] for keep, (_, got) in zip(keeps, parts)], others
 
 
-def reduce_packed(shares_one, shares_two, edges, finish):
+def reduce_packed(shares_one, shares_two, orders_one, orders_two, edges, finish):
     two, one = (
-        [[keep[:, first:last], got[:, first:last]] for first, last, _ in orders]
-        for keep, got, orders in (
-            (shares_two[0], swap(shares_two[1], "core"), ORDERS_TWO),
-            (shares_one[0], swap(shares_one[1], "core"), ORDERS_ONE),
-        )
-    )
-    names_two = list(zip(*(order for _, _, order in ORDERS_TWO)))
-    names_one = list(zip(*(order for _, _, order in ORDERS_ONE)))
+        [[shares[0], swap(shares[1], "core")]] for shares in (shares_two, shares_one)
+    )
+    names_two = list(zip(*(order for _, _, order in orders_two)))
+    names_one = list(zip(*(order for _, _, order in orders_one)))
     results = []
     halos = swap_halos(*edges)
     for step in range(2):
-        keeps, sends = add_terms(two)
+        keeps, sends = add_terms(two if step else cut(two, orders_two))
         one, sends = fence(one, sends)
         two = swaps(keeps, sends, names_two[step])
-        keeps, sends = add_terms(one)
+        keeps, sends = add_terms(one if step else cut(one, orders_one))
         one = swaps(keeps, sends, names_one[step])
         results.append(finish(step, sends, halos))
         two, results[-1] = fence(two, results[-1])
@@ -446,6 +448,8 @@
     def array(*shape, dtype=BF16):
         return jax.ShapeDtypeStruct(shape, dtype)
 
+    half = taps_in // slab_size // 2
+    orders_one, orders_two = portions_of(half, ORDERS_ONE), portions_of(half, ORDERS_TWO)
     if packed:
         shares = [array(16, taps_in // slab_size // 2, 128)] * 2
     else:
@@ -471,8 +475,8 @@
         pack_kernel,
         [edges, edges, array(16 * ROWS, 12 * ROWS), around, around],
         (send_lists, jnp.concatenate([features, cotangent])),
-        "sh",
-        [sem((2, 4))],
+        "hh",
+        [sem((2, 4)), pltpu.SMEM(send_lists.shape, jnp.int32), sem],
         limit=6,
     )
     got_first, got_second = swap_halos(first, second)
@@ -486,7 +490,7 @@
         flops=2 * product,
     )
     hidden, outer, outer_other, *shares_two = call(
-        functools.partial(forward_kernel, packed, ORDERS_TWO),
+        functools.partial(forward_kernel, packed, orders_two),
         [field, outer_shape, outer_shape] + shares,
         (
             table,
@@ -515,7 +519,7 @@
         flops=product,
     )
     shares_one = call(
-        functools.partial(backward_kernel, packed, ORDERS_ONE),
+        functools.partial(backward_kernel, packed, orders_one),
         shares,
         (inner, outer, grad_hidden),
         "vvv",
@@ -561,7 +565,7 @@
 
     if packed:
         terms, (output, grad_features) = reduce_packed(
-            shares_one, shares_two, (first, second), finish
+            shares_one, shares_two, orders_one, orders_two, (first, second), finish
         )
         out = array(channels // dp_size, taps_in // slab_size, dtype=F32)
         grad_one, grad_two = (

time: 78 us -> 77.5 us (level)
  transfers between devices with their start and end apart: 18 -> 18, of which waited for: 5 -> 4; matrix products, arithmetic and copies ran while one was open for 2% -> 1% of each run, Pallas kernels for 31% -> 31%
where the time goes in v2:
time: 77.5 us; the launch traced here: 77.3 us
  Pallas kernels  31.6 us (41%)
  starting transfers between devices  29.6 us (38%)
  waiting for transfers between devices  11.6 us (15%)
  other arithmetic  2 us (3%)
  between operations  1.62 us (2%)
  local copies, waits for them, and re-layouts  0.88 us (1%)
    pallas_call x9, Pallas kernels, call(): pl.pallas_call(kernel, out_shape=outs, in_specs=[pl.BlockSpec(memory_spac...  31.6 us
    ppermute x14, starting transfers between devices, swap(): lax.ppermute(array, ('dp', 'slab'), pair_perm(name, dp_size, slab_size))  20.8 us
    ppermute x14, waiting for transfers between devices, swap(): lax.ppermute(array, ('dp', 'slab'), pair_perm(name, dp_size, slab_size))  11.6 us
    ppermute x2, starting transfers between devices, swap_halos(): lax.ppermute(first, 'slab', even)  7.36 us
  transfers between devices with their start and end apart: 18, of which 4 were waited for; matrix products, arithmetic and copies ran while one was open for 1% of the time, Pallas kernels for 31%

profile of v2, /device:TPU:0, one launch (start us, length us, event | category | flops | bytes accessed | tf_op | source)
XLA Modules:
  0.0 77.3 jit_solution(7993438394654202248)
XLA Ops:
  0.6 1.1 %pad_maximum_fusion.fields = bf16[2,10,64,256]{3,2,1,0:T(8,128)(2,1)S(1)} fusion(bf16[1,10,64,256]{3,2,1,0:T(8,128)(2,1)} %rows.3, bf16[1,10,64,256]{3,2,1,0:T(8,128)(2,1)} %rows.2), kind=kLoop, calls=%fused_computation | loop fusion | flops 327680 | bytes 1310720 | tf_op jit(solution)/shard_map/concatenate | solution.py:477
  1.8 0.7 copy-done.2
  2.5 0.7 shard_map.102
  3.1 3.0 %collective-permute-start = (bf16[2,16,512]{2,1,0:T(8,128)(2,1)S(1)}, bf16[2,16,512]{2,1,0:T(8,128)(2,1)S(1)}, u32[]{:S(2)}, u32[]{:S(2)}) collective-permute-start(bf16[2,16,512]{2,1,0:T(8,128)(2,1)S(1)} %get-tuple-element.45), channel_id=1, source_target_pairs={{0,1},{1,0},{2,3},{3,2},{4,5},{5,4},{6,7},{7,6},{8,9},{9,8},{10,11... | collective-permute-start | bytes 98312 | tf_op jit(solution)/shard_map/ppermute | solution.py:75
  6.1 0.7 collective-permute-start.1
  6.8 4.8 %shard_map.103 = (bf16[9,640,256]{2,1,0:T(8,128)(2,1)S(1)}, bf16[9,640,256]{2,1,0:T(8,128)(2,1)S(1)}, f32[640,256]{1,0:T(8,128)S(1)}, bf16[6912,256]{1,0:T(8,128)(2,1)S(1)}) custom-call(s32[10,1,27]{2,1,0:T(1,128)S(1)} %bitcast.11, bf16[4,15,16,256]{3,2,1,0:T(8,128)(2,1)S(1)} %get-tuple-element.43.planes.source, ...), custom_call_target="tpu_custom_call" | custom-call | flops 4529848320 | tf_op jit(solution)/shard_map/pallas_call | solution.py:368
  11.7 6.0 %shard_map.104 = (bf16[4,10,16,256]{3,2,1,0:T(8,128)(2,1)S(1)}, bf16[9,320,256]{2,1,0:T(8,128)(2,1)S(1)}, bf16[9,320,256]{2,1,0:T(8,128)(2,1)S(1)}, bf16[16,432,...) custom-call(s32[10,1,27]{2,1,0:T(1,128)S(1)} %bitcast.12, bf16[4,15,16,256]{3,2,1,0:T(8,128)(2,1)S(1)} %get-tuple-element.43.planes.source, ...), custom_call_target="tpu_custom_call" | custom-call | flops 4529848320 | tf_op jit(solution)/shard_map/pallas_call | solution.py:368
  17.8 3.0 %shard_map.105 = (bf16[4,10,16,256]{3,2,1,0:T(8,128)(2,1)S(1)}, bf16[2,16,512]{2,1,0:T(8,128)(2,1)S(1)}, bf16[2,16,512]{2,1,0:T(8,128)(2,1)S(1)}) custom-call(s32[1,1,2,2]{3,2,1,0:T(2,128)S(1)} %copy-done.3, bf16[9,640,256]{2,1,0:T(8,128)(2,1)S(1)} %get-tuple-element.50.other.inner, bf16[9,320,256]{2,1,0:T(8,128)(2,1)S(1)} %get-tuple-element.55.outer, ...), custom_call_target="tpu_custom_call" | custom-call | flops 2264924160 | tf_op jit(solution)/shard_map/pallas_call | solution.py:368
  20.8 3.4 %shard_map.106 = (bf16[16,432,128]{2,1,0:T(8,128)(2,1)S(1)}, bf16[16,432,128]{2,1,0:T(8,128)(2,1)S(1)}) custom-call(bf16[9,640,256]{2,1,0:T(8,128)(2,1)S(1)} %get-tuple-element.49.inner, bf16[9,320,256]{2,1,0:T(8,128)(2,1)S(1)} %get-tuple-element.58.outer, bf16[4,10,16,256]{3,2,1,0:T(8,128)(2,1)S(1)} %get-tuple-element.59.grad_hidden.source), custom_call_target="tpu_custom_call" | custom-call | flops 2264924160 | tf_op jit(solution)/shard_map/pallas_call | solution.py:368
  24.3 0.5 collective-permute-start.5
  25.5 4.4 %collective-permute-start.3 = (bf16[2,16,512]{2,1,0:T(8,128)(2,1)S(1)}, bf16[2,16,512]{2,1,0:T(8,128)(2,1)S(1)}, u32[]{:S(2)}, u32[]{:S(2)}) collective-permute-start(bf16[2,16,512]{2,1,0:T(8,128)(2,1)S(1)} %get-tuple-element.56), channel_id=1, source_target_pairs={{0,1},{1,0},{2,3},{3,2},{4,5},{5,4},{6,7},{7,6},{8,9},{9,8},{10,11... | collective-permute-start | bytes 98312 | tf_op jit(solution)/shard_map/ppermute | solution.py:75
  29.8 0.8 %collective-permute-start.4 = (bf16[2,16,512]{2,1,0:T(8,128)(2,1)S(1)}, bf16[2,16,512]{2,1,0:T(8,128)(2,1)S(1)}, u32[]{:S(2)}, u32[]{:S(2)}) collective-permute-start(bf16[2,16,512]{2,1,0:T(8,128)(2,1)S(1)} %get-tuple-element.57), channel_id=1, source_target_pairs={{1,2},{2,1},{3,4},{4,3},{5,6},{6,5},{9,10},{10,9},{11,12},{12,11},... | collective-permute-start | bytes 98312 | tf_op jit(solution)/shard_map/ppermute | solution.py:75
  30.9 1.6 %collective-permute-start.7 = (bf16[8,176,128]{2,1,0:T(8,128)(2,1)S(1)}, bf16[8,176,128]{2,1,0:T(8,128)(2,1)S(1)}, u32[]{:S(2)}, u32[]{:S(2)}) collective-permute-start(bf16[8,176,128]{2,1,0:T(8,128)(2,1)S(1)} %get-tuple-element.67), channel_id=1, source_target_pairs={{0,16},{1,17},{2,18},{3,19},{4,20},{5,21},{6,22},{7,23},{8,24},{9,... | collective-permute-start | bytes 1081352 | tf_op jit(solution)/shard_map/ppermute | solution.py:68
  32.5 4.3 %collective-permute-start.6 = (bf16[8,256,128]{2,1,0:T(8,128)(2,1)S(1)}, bf16[8,256,128]{2,1,0:T(8,128)(2,1)S(1)}, u32[]{:S(2)}, u32[]{:S(2)}) collective-permute-start(bf16[8,256,128]{2,1,0:T(8,128)(2,1)S(1)} %get-tuple-element.65), channel_id=1, source_target_pairs={{0,1},{1,0},{2,3},{3,2},{4,5},{5,4},{6,7},{7,6},{8,9},{9,8},{10,11... | collective-permute-start | bytes 1572872 | tf_op jit(solution)/shard_map/ppermute | solution.py:68
  36.9 0.6 collective-permute-start.9
  37.6 1.7 %collective-permute-start.8 = (bf16[8,288,128]{2,1,0:T(8,128)(2,1)S(1)}, bf16[8,288,128]{2,1,0:T(8,128)(2,1)S(1)}, u32[]{:S(2)}, u32[]{:S(2)}) collective-permute-start(bf16[8,288,128]{2,1,0:T(8,128)(2,1)S(1)} %get-tuple-element.85.rest_0_), channel_id=1, source_target_pairs={{0,2},{1,3},{2,0},{3,1},{4,6},{5,7},{6,4},{7,5},{8,10},{9,11},{10,... | collective-permute-start | bytes 1769480 | tf_op jit(solution)/shard_map/ppermute | solution.py:68
  39.3 5.8 %shard_map.107 = bf16[1,10,64,256]{3,2,1,0:T(8,128)(2,1)} custom-call(s32[10,1,27]{2,1,0:T(1,128)S(1)} %bitcast.13, s32[1,1]{1,0:T(1,128)S(6)} %copy.15.counts, bf16[4,10,16,256]{3,2,1,0:T(8,128)(2,1)S(1)} %get-tuple-element.54.hidden.source, bf16[2,16,512]{2,1,0:T(8,128)(2,1)S(1)} %collective-permute-done.3.got_first, ...), custom_call_target="tpu_custom_call" | custom-call | flops 2264924160 | tf_op jit(solution)/shard_map/pallas_call | solution.py:368
  45.2 2.9 %collective-permute-done.6 = bf16[8,256,128]{2,1,0:T(8,128)(2,1)S(1)} collective-permute-done((bf16[8,256,128]{2,1,0:T(8,128)(2,1)S(1)}, bf16[8,256,128]{2,1,0:T(8,128)(2,1)S(1)}, u32[]{:S(2)}, u32[]{:S(2)}) %collective-permute-start.6) | collective-permute-done | bytes 524320 | tf_op jit(solution)/shard_map/ppermute | solution.py:68
  48.1 0.6 collective-permute-start.10
  48.7 1.7 %collective-permute-start.11 = (bf16[4,176,128]{2,1,0:T(8,128)(2,1)S(1)}, bf16[4,176,128]{2,1,0:T(8,128)(2,1)S(1)}, u32[]{:S(2)}, u32[]{:S(2)}) collective-permute-start(bf16[4,176,128]{2,1,0:T(8,128)(2,1)S(1)} %get-tuple-element.74), channel_id=1, source_target_pairs={{0,1},{1,0},{2,3},{3,2},{4,5},{5,4},{6,7},{7,6},{8,9},{9,8},{10,11... | collective-permute-start | bytes 540680 | tf_op jit(solution)/shard_map/ppermute | solution.py:68
  50.5 1.7 %collective-permute-start.13 = (bf16[4,144,128]{2,1,0:T(8,128)(2,1)S(1)}, bf16[4,144,128]{2,1,0:T(8,128)(2,1)S(1)}, u32[]{:S(2)}, u32[]{:S(2)}) collective-permute-start(bf16[4,144,128]{2,1,0:T(8,128)(2,1)S(1)} %get-tuple-element.101.rest_1_), channel_id=1, source_target_pairs={{0,2},{1,3},{2,0},{3,1},{4,6},{5,7},{6,4},{7,5},{8,10},{9,11},{10,... | collective-permute-start | bytes 442376 | tf_op jit(solution)/shard_map/ppermute | solution.py:68
  52.2 1.6 %collective-permute-start.12 = (bf16[4,288,128]{2,1,0:T(8,128)(2,1)S(1)}, bf16[4,288,128]{2,1,0:T(8,128)(2,1)S(1)}, u32[]{:S(2)}, u32[]{:S(2)}) collective-permute-start(bf16[4,288,128]{2,1,0:T(8,128)(2,1)S(1)} %get-tuple-element.91.rest_0_), channel_id=1, source_target_pairs={{0,16},{1,17},{2,18},{3,19},{4,20},{5,21},{6,22},{7,23},{8,24},{9,... | collective-permute-start | bytes 884744 | tf_op jit(solution)/shard_map/ppermute | solution.py:68
  53.8 5.8 %shard_map.108 = bf16[1,10,64,256]{3,2,1,0:T(8,128)(2,1)} custom-call(s32[10,1,27]{2,1,0:T(1,128)S(1)} %bitcast.14, s32[1,1]{1,0:T(1,128)S(6)} %copy.15.counts, bf16[4,10,16,256]{3,2,1,0:T(8,128)(2,1)S(1)} %get-tuple-element.59.grad_hidden.source, bf16[2,16,512]{2,1,0:T(8,128)(2,1)S(1)} %collective-permute-done.3.got_first, ...), custom_call_target="tpu_custom_call" | custom-call | flops 2264924160 | tf_op jit(solution)/shard_map/pallas_call | solution.py:368
  59.9 1.6 %collective-permute-start.14 = (bf16[2,432,128]{2,1,0:T(8,128)(2,1)S(1)}, bf16[2,432,128]{2,1,0:T(8,128)(2,1)S(1)}, u32[]{:S(2)}, u32[]{:S(2)}) collective-permute-start(bf16[2,432,128]{2,1,0:T(8,128)(2,1)S(1)} %get-tuple-element.78), channel_id=1, source_target_pairs={{0,2},{1,3},{2,0},{3,1},{4,6},{5,7},{6,4},{7,5},{8,10},{9,11},{10,... | collective-permute-start | bytes 663560 | tf_op jit(solution)/shard_map/ppermute | solution.py:68
  61.7 1.8 %collective-permute-start.15 = (bf16[2,432,128]{2,1,0:T(8,128)(2,1)S(1)}, bf16[2,432,128]{2,1,0:T(8,128)(2,1)S(1)}, u32[]{:S(2)}, u32[]{:S(2)}) collective-permute-start(bf16[2,432,128]{2,1,0:T(8,128)(2,1)S(1)} %get-tuple-element.80), channel_id=1, source_target_pairs={{0,1},{1,0},{2,3},{3,2},{4,5},{5,4},{6,7},{7,6},{8,9},{9,8},{10,11... | collective-permute-start | bytes 663560 | tf_op jit(solution)/shard_map/ppermute | solution.py:68
  63.5 3.5 %collective-permute-done.14 = bf16[2,432,128]{2,1,0:T(8,128)(2,1)S(1)} collective-permute-done((bf16[2,432,128]{2,1,0:T(8,128)(2,1)S(1)}, bf16[2,432,128]{2,1,0:T(8,128)(2,1)S(1)}, u32[]{:S(2)}, u32[]{:S(2)}) %collective-permute-start.14) | collective-permute-done | bytes 221216 | tf_op jit(solution)/shard_map/ppermute | solution.py:68
  67.1 1.8 %collective-permute-start.17 = (bf16[1,432,128]{2,1,0:T(8,128)(2,1)S(1)}, bf16[1,432,128]{2,1,0:T(8,128)(2,1)S(1)}, u32[]{:S(2)}, u32[]{:S(2)}) collective-permute-start(bf16[1,432,128]{2,1,0:T(8,128)(2,1)S(1)} %get-tuple-element.81), channel_id=1, source_target_pairs={{0,4},{1,5},{2,6},{3,7},{4,0},{5,1},{6,2},{7,3},{8,12},{9,13},{10,... | collective-permute-start | bytes 331784 | tf_op jit(solution)/shard_map/ppermute | solution.py:68
  68.9 1.3 %collective-permute-start.16 = (bf16[1,432,128]{2,1,0:T(8,128)(2,1)S(1)}, bf16[1,432,128]{2,1,0:T(8,128)(2,1)S(1)}, u32[]{:S(2)}, u32[]{:S(2)}) collective-permute-start(bf16[1,432,128]{2,1,0:T(8,128)(2,1)S(1)} %get-tuple-element.104), channel_id=1, source_target_pairs={{0,4},{1,5},{2,6},{3,7},{4,0},{5,1},{6,2},{7,3},{8,12},{9,13},{10,... | collective-permute-start | bytes 331784 | tf_op jit(solution)/shard_map/ppermute | solution.py:68
  70.1 5.0 %collective-permute-done.17 = bf16[1,432,128]{2,1,0:T(8,128)(2,1)S(1)} collective-permute-done((bf16[1,432,128]{2,1,0:T(8,128)(2,1)S(1)}, bf16[1,432,128]{2,1,0:T(8,128)(2,1)S(1)}, u32[]{:S(2)}, u32[]{:S(2)}) %collective-permute-start.17) | collective-permute-done | bytes 110624 | tf_op jit(solution)/shard_map/ppermute | solution.py:68
  75.1 1.0 %shard_map.110 = f32[64,864]{1,0:T(8,128)} custom-call(bf16[432,128]{1,0:T(8,128)(2,1)S(1)} %get-tuple-element.102.keep, bf16[432,128]{1,0:T(8,128)(2,1)S(1)} %bitcast.9), custom_call_target="tpu_custom_call" | custom-call | tf_op jit(solution)/shard_map/pallas_call | solution.py:368
  76.1 0.2 collective-permute-done.16
  76.3 1.0 %shard_map.109 = f32[64,864]{1,0:T(8,128)} custom-call(bf16[432,128]{1,0:T(8,128)(2,1)S(1)} %get-tuple-element.105.keep, bf16[432,128]{1,0:T(8,128)(2,1)S(1)} %bitcast.10), custom_call_target="tpu_custom_call" | custom-call | tf_op jit(solution)/shard_map/pallas_call | solution.py:368
  (48 shorter events, 1.2 us)
Async XLA Ops:
  0.6 6.2 %copy-start.6 = (s32[1,10,27]{2,0,1:T(1,128)S(1)}, s32[1,10,27]{2,0,1:T(1,128)}, u32[]{:S(2)}) copy-start(s32[1,10,27]{2,0,1:T(1,128)} %param.9) | copy-start | bytes 3244
  1.8 0.7 copy-start.2
  3.1 8.5 %collective-permute-start = (bf16[2,16,512]{2,1,0:T(8,128)(2,1)S(1)}, bf16[2,16,512]{2,1,0:T(8,128)(2,1)S(1)}, u32[]{:S(2)}, u32[]{:S(2)}) collective-permute-start(bf16[2,16,512]{2,1,0:T(8,128)(2,1)S(1)} %get-tuple-element.45), channel_id=1, source_target_pairs={{0,1},{1,0},{2,3},{3,2},{4,5},{5,4},{6,7},{7,6},{8,9},{9,8},{10,11... | collective-permute-start | bytes 98312 | tf_op jit(solution)/shard_map/ppermute | solution.py:75
  6.1 5.5 %collective-permute-start.1 = (bf16[2,16,512]{2,1,0:T(8,128)(2,1)S(1)}, bf16[2,16,512]{2,1,0:T(8,128)(2,1)S(1)}, u32[]{:S(2)}, u32[]{:S(2)}) collective-permute-start(bf16[2,16,512]{2,1,0:T(8,128)(2,1)S(1)} %get-tuple-element.46), channel_id=1, source_target_pairs={{1,2},{2,1},{3,4},{4,3},{5,6},{6,5},{9,10},{10,9},{11,12},{12,11},... | collective-permute-start | bytes 98312 | tf_op jit(solution)/shard_map/ppermute | solution.py:75
  11.7 6.1 %copy-start.3 = (s32[1,1,2,2]{3,2,1,0:T(2,128)S(1)}, s32[1,1,2,2]{3,2,1,0:T(2,128)}, u32[]{:S(2)}) copy-start(s32[1,1,2,2]{3,2,1,0:T(2,128)} %lists.1) | copy-start | bytes 52
  11.7 6.1 %copy-start.4 = (bf16[6912,256]{1,0:T(8,128)(2,1)S(1)}, bf16[6912,256]{1,0:T(8,128)(2,1)}, u32[]{:S(2)}) copy-start(bf16[6912,256]{1,0:T(8,128)(2,1)} %weight.6) | copy-start | bytes 10616836
  17.7 12.9 %collective-permute-start.2 = (bf16[16,432,128]{2,1,0:T(8,128)(2,1)S(1)}, bf16[16,432,128]{2,1,0:T(8,128)(2,1)S(1)}, u32[]{:S(2)}, u32[]{:S(2)}) collective-permute-start(bf16[16,432,128]{2,1,0:T(8,128)(2,1)S(1)} %get-tuple-element.53), channel_id=1, source_target_pairs={{0,8},{1,9},{2,10},{3,11},{4,12},{5,13},{6,14},{7,15},{8,0},{9,1},... | collective-permute-start | bytes 5308424 | tf_op jit(solution)/shard_map/ppermute | solution.py:68
  24.3 12.5 %collective-permute-start.5 = (bf16[16,432,128]{2,1,0:T(8,128)(2,1)S(1)}, bf16[16,432,128]{2,1,0:T(8,128)(2,1)S(1)}, u32[]{:S(2)}, u32[]{:S(2)}) collective-permute-start(bf16[16,432,128]{2,1,0:T(8,128)(2,1)S(1)} %get-tuple-element.62), channel_id=1, source_target_pairs={{0,8},{1,9},{2,10},{3,11},{4,12},{5,13},{6,14},{7,15},{8,0},{9,1},... | collective-permute-start | bytes 5308424 | tf_op jit(solution)/shard_map/ppermute | solution.py:68
  25.5 12.1 %collective-permute-start.3 = (bf16[2,16,512]{2,1,0:T(8,128)(2,1)S(1)}, bf16[2,16,512]{2,1,0:T(8,128)(2,1)S(1)}, u32[]{:S(2)}, u32[]{:S(2)}) collective-permute-start(bf16[2,16,512]{2,1,0:T(8,128)(2,1)S(1)} %get-tuple-element.56), channel_id=1, source_target_pairs={{0,1},{1,0},{2,3},{3,2},{4,5},{5,4},{6,7},{7,6},{8,9},{9,8},{10,11... | collective-permute-start | bytes 98312 | tf_op jit(solution)/shard_map/ppermute | solution.py:75
  29.8 9.5 %collective-permute-start.4 = (bf16[2,16,512]{2,1,0:T(8,128)(2,1)S(1)}, bf16[2,16,512]{2,1,0:T(8,128)(2,1)S(1)}, u32[]{:S(2)}, u32[]{:S(2)}) collective-permute-start(bf16[2,16,512]{2,1,0:T(8,128)(2,1)S(1)} %get-tuple-element.57), channel_id=1, source_target_pairs={{1,2},{2,1},{3,4},{4,3},{5,6},{6,5},{9,10},{10,9},{11,12},{12,11},... | collective-permute-start | bytes 98312 | tf_op jit(solution)/shard_map/ppermute | solution.py:75
  30.9 14.2 %collective-permute-start.7 = (bf16[8,176,128]{2,1,0:T(8,128)(2,1)S(1)}, bf16[8,176,128]{2,1,0:T(8,128)(2,1)S(1)}, u32[]{:S(2)}, u32[]{:S(2)}) collective-permute-start(bf16[8,176,128]{2,1,0:T(8,128)(2,1)S(1)} %get-tuple-element.67), channel_id=1, source_target_pairs={{0,16},{1,17},{2,18},{3,19},{4,20},{5,21},{6,22},{7,23},{8,24},{9,... | collective-permute-start | bytes 1081352 | tf_op jit(solution)/shard_map/ppermute | solution.py:68
  32.5 15.6 %collective-permute-start.6 = (bf16[8,256,128]{2,1,0:T(8,128)(2,1)S(1)}, bf16[8,256,128]{2,1,0:T(8,128)(2,1)S(1)}, u32[]{:S(2)}, u32[]{:S(2)}) collective-permute-start(bf16[8,256,128]{2,1,0:T(8,128)(2,1)S(1)} %get-tuple-element.65), channel_id=1, source_target_pairs={{0,1},{1,0},{2,3},{3,2},{4,5},{5,4},{6,7},{7,6},{8,9},{9,8},{10,11... | collective-permute-start | bytes 1572872 | tf_op jit(solution)/shard_map/ppermute | solution.py:68
  36.9 2.4 %copy-start = (bf16[1,10,64,256]{3,2,1,0:T(8,128)(2,1)S(1)}, bf16[1,10,64,256]{3,2,1,0:T(8,128)(2,1)}, u32[]{:S(2)}) copy-start(bf16[1,10,64,256]{3,2,1,0:T(8,128)(2,1)} %rows.2) | copy-start | bytes 983044
  36.9 13.6 %collective-permute-start.9 = (bf16[8,144,128]{2,1,0:T(8,128)(2,1)S(1)}, bf16[8,144,128]{2,1,0:T(8,128)(2,1)S(1)}, u32[]{:S(2)}, u32[]{:S(2)}) collective-permute-start(bf16[8,144,128]{2,1,0:T(8,128)(2,1)S(1)} %get-tuple-element.83.rest_1_), channel_id=1, source_target_pairs={{0,16},{1,17},{2,18},{3,19},{4,20},{5,21},{6,22},{7,23},{8,24},{9,... | collective-permute-start | bytes 884744 | tf_op jit(solution)/shard_map/ppermute | solution.py:68
  37.6 14.5 %collective-permute-start.8 = (bf16[8,288,128]{2,1,0:T(8,128)(2,1)S(1)}, bf16[8,288,128]{2,1,0:T(8,128)(2,1)S(1)}, u32[]{:S(2)}, u32[]{:S(2)}) collective-permute-start(bf16[8,288,128]{2,1,0:T(8,128)(2,1)S(1)} %get-tuple-element.85.rest_0_), channel_id=1, source_target_pairs={{0,2},{1,3},{2,0},{3,1},{4,6},{5,7},{6,4},{7,5},{8,10},{9,11},{10,... | collective-permute-start | bytes 1769480 | tf_op jit(solution)/shard_map/ppermute | solution.py:68
  45.2 8.7 %copy-start.1 = (bf16[1,10,64,256]{3,2,1,0:T(8,128)(2,1)S(1)}, bf16[1,10,64,256]{3,2,1,0:T(8,128)(2,1)}, u32[]{:S(2)}) copy-start(bf16[1,10,64,256]{3,2,1,0:T(8,128)(2,1)} %rows.3) | copy-start | bytes 983044
  45.2 8.7 %copy-start.5 = (bf16[6912,256]{1,0:T(8,128)(2,1)S(1)}, bf16[6912,256]{1,0:T(8,128)(2,1)}, u32[]{:S(2)}) copy-start(bf16[6912,256]{1,0:T(8,128)(2,1)} %weight.7) | copy-start | bytes 10616836
  48.1 11.6 %collective-permute-start.10 = (bf16[4,256,128]{2,1,0:T(8,128)(2,1)S(1)}, bf16[4,256,128]{2,1,0:T(8,128)(2,1)S(1)}, u32[]{:S(2)}, u32[]{:S(2)}) collective-permute-start(bf16[4,256,128]{2,1,0:T(8,128)(2,1)S(1)} %get-tuple-element.73), channel_id=1, source_target_pairs={{0,16},{1,17},{2,18},{3,19},{4,20},{5,21},{6,22},{7,23},{8,24},{9,... | collective-permute-start | bytes 786440 | tf_op jit(solution)/shard_map/ppermute | solution.py:68
  48.7 11.0 %collective-permute-start.11 = (bf16[4,176,128]{2,1,0:T(8,128)(2,1)S(1)}, bf16[4,176,128]{2,1,0:T(8,128)(2,1)S(1)}, u32[]{:S(2)}, u32[]{:S(2)}) collective-permute-start(bf16[4,176,128]{2,1,0:T(8,128)(2,1)S(1)} %get-tuple-element.74), channel_id=1, source_target_pairs={{0,1},{1,0},{2,3},{3,2},{4,5},{5,4},{6,7},{7,6},{8,9},{9,8},{10,11... | collective-permute-start | bytes 540680 | tf_op jit(solution)/shard_map/ppermute | solution.py:68
  50.5 11.1 %collective-permute-start.13 = (bf16[4,144,128]{2,1,0:T(8,128)(2,1)S(1)}, bf16[4,144,128]{2,1,0:T(8,128)(2,1)S(1)}, u32[]{:S(2)}, u32[]{:S(2)}) collective-permute-start(bf16[4,144,128]{2,1,0:T(8,128)(2,1)S(1)} %get-tuple-element.101.rest_1_), channel_id=1, source_target_pairs={{0,2},{1,3},{2,0},{3,1},{4,6},{5,7},{6,4},{7,5},{8,10},{9,11},{10,... | collective-permute-start | bytes 442376 | tf_op jit(solution)/shard_map/ppermute | solution.py:68
  52.2 9.3 %collective-permute-start.12 = (bf16[4,288,128]{2,1,0:T(8,128)(2,1)S(1)}, bf16[4,288,128]{2,1,0:T(8,128)(2,1)S(1)}, u32[]{:S(2)}, u32[]{:S(2)}) collective-permute-start(bf16[4,288,128]{2,1,0:T(8,128)(2,1)S(1)} %get-tuple-element.91.rest_0_), channel_id=1, source_target_pairs={{0,16},{1,17},{2,18},{3,19},{4,20},{5,21},{6,22},{7,23},{8,24},{9,... | collective-permute-start | bytes 884744 | tf_op jit(solution)/shard_map/ppermute | solution.py:68
  59.9 7.2 %collective-permute-start.14 = (bf16[2,432,128]{2,1,0:T(8,128)(2,1)S(1)}, bf16[2,432,128]{2,1,0:T(8,128)(2,1)S(1)}, u32[]{:S(2)}, u32[]{:S(2)}) collective-permute-start(bf16[2,432,128]{2,1,0:T(8,128)(2,1)S(1)} %get-tuple-element.78), channel_id=1, source_target_pairs={{0,2},{1,3},{2,0},{3,1},{4,6},{5,7},{6,4},{7,5},{8,10},{9,11},{10,... | collective-permute-start | bytes 663560 | tf_op jit(solution)/shard_map/ppermute | solution.py:68
  61.7 7.2 %collective-permute-start.15 = (bf16[2,432,128]{2,1,0:T(8,128)(2,1)S(1)}, bf16[2,432,128]{2,1,0:T(8,128)(2,1)S(1)}, u32[]{:S(2)}, u32[]{:S(2)}) collective-permute-start(bf16[2,432,128]{2,1,0:T(8,128)(2,1)S(1)} %get-tuple-element.80), channel_id=1, source_target_pairs={{0,1},{1,0},{2,3},{3,2},{4,5},{5,4},{6,7},{7,6},{8,9},{9,8},{10,11... | collective-permute-start | bytes 663560 | tf_op jit(solution)/shard_map/ppermute | solution.py:68
  67.1 8.1 %collective-permute-start.17 = (bf16[1,432,128]{2,1,0:T(8,128)(2,1)S(1)}, bf16[1,432,128]{2,1,0:T(8,128)(2,1)S(1)}, u32[]{:S(2)}, u32[]{:S(2)}) collective-permute-start(bf16[1,432,128]{2,1,0:T(8,128)(2,1)S(1)} %get-tuple-element.81), channel_id=1, source_target_pairs={{0,4},{1,5},{2,6},{3,7},{4,0},{5,1},{6,2},{7,3},{8,12},{9,13},{10,... | collective-permute-start | bytes 331784 | tf_op jit(solution)/shard_map/ppermute | solution.py:68
  68.9 7.5 %collective-permute-start.16 = (bf16[1,432,128]{2,1,0:T(8,128)(2,1)S(1)}, bf16[1,432,128]{2,1,0:T(8,128)(2,1)S(1)}, u32[]{:S(2)}, u32[]{:S(2)}) collective-permute-start(bf16[1,432,128]{2,1,0:T(8,128)(2,1)S(1)} %get-tuple-element.104), channel_id=1, source_target_pairs={{0,4},{1,5},{2,6},{3,7},{4,0},{5,1},{6,2},{7,3},{8,12},{9,13},{10,... | collective-permute-start | bytes 331784 | tf_op jit(solution)/shard_map/ppermute | solution.py:68
